TPU v7x, 32 devices: a whole 2x2x4 slice. The times are simulated.
32 devices in a mesh: wide: 8 (over y, x, core), narrow: 4 (over z).
Axes of the slice: x: 2, y: 2, z: 4, core: 2. Of those that a mesh axis runs over, the one named last changes fastest.
Arguments:
- tokens: bfloat16 [16384, 1024], P(('wide', 'narrow')), may hold values from -6 to 6
- w_query: bfloat16 [1024, 1024], P(('wide', 'narrow')), may hold values from -0.0234375 to 0.0234375
- w_key: bfloat16 [1024, 1024], P(('wide', 'narrow')), may hold values from -0.1875 to 0.1875
- w_value: bfloat16 [1024, 1024], P(('wide', 'narrow')), may hold values from -0.1875 to 0.1875
- w_output: bfloat16 [1024, 1024], P(('wide', 'narrow')), may hold values from -1.5 to 1.5
- w_gate: bfloat16 [1024, 2816], P(('wide', 'narrow')), may hold values from -0.1875 to 0.1875
- w_up: bfloat16 [1024, 2816], P(('wide', 'narrow')), may hold values from -0.1875 to 0.1875
- w_down: bfloat16 [2816, 1024], P(('wide', 'narrow')), may hold values from -0.109375 to 0.109375
- gain_attn: bfloat16 [1024], P(('wide', 'narrow')), may hold values from 0.5 to 1.5
- gain_ffn: bfloat16 [1024], P(('wide', 'narrow')), may hold values from 0.5 to 1.5
- rel_table: bfloat16 [512], P(('wide', 'narrow')), may hold values from -4 to 4
- lay_table: bfloat16 [512], P(('wide', 'narrow')), may hold values from -4 to 4
- ocr_counts: int32 [32], P(('wide', 'narrow')), may hold values from 50 to 316, as said below
- rel_bucket: int32 [16384, 512], P(('wide', 'narrow')), may hold values from 0 to 31
- lay_bucket: int32 [16384, 512], P(('wide', 'narrow')), may hold values from 0 to 31
- cotangent: bfloat16 [16384, 1024], P(('wide', 'narrow')), may hold values from -6 to 6
Outputs:
- output: bfloat16 [16384, 1024], P(('wide', 'narrow'))
- grad_tokens: float32 [16384, 1024], P(('wide', 'narrow'))
- grad_query: float32 [1024, 1024], P(('wide', 'narrow'))
- grad_key: float32 [1024, 1024], P(('wide', 'narrow'))
- grad_value: float32 [1024, 1024], P(('wide', 'narrow'))
- grad_output: float32 [1024, 1024], P(('wide', 'narrow'))
- grad_gate: float32 [1024, 2816], P(('wide', 'narrow'))
- grad_up: float32 [1024, 2816], P(('wide', 'narrow'))
- grad_down: float32 [2816, 1024], P(('wide', 'narrow'))
- grad_gain_attn: float32 [1024], P(('wide', 'narrow'))
- grad_gain_ffn: float32 [1024], P(('wide', 'narrow'))
- grad_rel: float32 [512], P(('wide', 'narrow'))
- grad_lay: float32 [512], P(('wide', 'narrow'))
Inputs may be any that keep to these rules, and one draw needn't show every extreme that they name: `ocr_counts`: one page in every draw holds exactly 316 OCR tokens.
All inputs are finite; a program needn't handle non-finite values.
Results may differ from a plain program's by a relative error of at most 0.035.
Values may be sent and summed in bfloat16 or wider, within the bound.
A program may use at most 320 MiB of HBM per device.

v0:
```python
import functools

import jax
import jax.numpy as jnp
from jax import lax
from jax.experimental import pallas as pl
from jax.experimental.pallas import tpu as pltpu
from jax.sharding import PartitionSpec as P

H = 16
HD = 64
NB = 32
IMG = 196
RING = 6
SCATTER_COPIES = 10
LAG = (0, 1, 2, 4, 8)
LINE_RING = 10
FEW_LAG = (0, 1, 2, 4, 14)
LAGS = LAG[-1]
FFN_LAG = 6
LATE = 2
BACK_QB = 16
WIDE = 512
DOWN_PIECE = 256
REST = 512
UP_TILES = 6
TILE = 256
QB = 8
GELU_SCALE = 0.7978845608028654
GELU_CUBE = 0.044715


RMS_EPSILON = 1e-06
MASK_SCORE = -1000000000.0
HEAD_GROUP = 4


def rms_scale(values, gain):
    return (
        values * lax.rsqrt(jnp.mean(values * values, axis=-1, keepdims=True) + RMS_EPSILON) * gain
    )


def gated_product(gate_act, up_proj):
    return jax.nn.gelu(gate_act, approximate=True) * up_proj


def product(left, right):
    return jnp.dot(left, right, preferred_element_type=jnp.float32)


def contract_rows(left, right):
    return lax.dot_general(
        left, right, (((0,), (0,)), ((), ())), preferred_element_type=jnp.float32
    )


def contract_cols(left, right):
    return lax.dot_general(
        left, right, (((1,), (1,)), ((), ())), preferred_element_type=jnp.float32
    )


def split_heads(matrix):
    return jnp.moveaxis(matrix.reshape(matrix.shape[0], H // HEAD_GROUP, HEAD_GROUP, HD), 1, 0)


def join_heads(stacked):
    return jnp.moveaxis(stacked, 0, 1).reshape(stacked.shape[1], H * HD)


def group_tables(table_all):
    return jnp.moveaxis(table_all.reshape(2 * NB, H // HEAD_GROUP, HEAD_GROUP), 1, 0)


def group_scores(query_group, key_group, table_group, onehot, valid):
    scores = jnp.einsum("ihd,jhd->hij", query_group, key_group, preferred_element_type=jnp.float32)
    scores = scores + jnp.einsum(
        "ijb,bh->hij", onehot, table_group, preferred_element_type=jnp.float32
    )
    return jnp.where(valid[None, None, :], scores, MASK_SCORE)


def gather_weights(
    w_query,
    w_key,
    w_value,
    w_output,
    w_gate,
    w_up,
    w_down,
    gain_attn,
    gain_ffn,
    rel_table,
    lay_table,
):
    return (
        lax.all_gather(w_query, ("wide", "narrow"), axis=0, tiled=True),
        lax.all_gather(w_key, ("wide", "narrow"), axis=0, tiled=True),
        lax.all_gather(w_value, ("wide", "narrow"), axis=0, tiled=True),
        lax.all_gather(w_output, ("wide", "narrow"), axis=0, tiled=True),
        lax.all_gather(w_gate, ("wide", "narrow"), axis=0, tiled=True),
        lax.all_gather(w_up, ("wide", "narrow"), axis=0, tiled=True),
        lax.all_gather(w_down, ("wide", "narrow"), axis=0, tiled=True),
        lax.all_gather(gain_attn, ("wide", "narrow"), axis=0, tiled=True),
        lax.all_gather(gain_ffn, ("wide", "narrow"), axis=0, tiled=True),
        lax.all_gather(rel_table, ("wide", "narrow"), axis=0, tiled=True),
        lax.all_gather(lay_table, ("wide", "narrow"), axis=0, tiled=True),
    )


def table_pair(full_rel, full_lay):
    return jnp.concatenate([full_rel.reshape(NB, H), full_lay.reshape(NB, H)], axis=0)


def forward_pass(tokens_f, weights, onehot, valid):
    (
        full_query,
        full_key,
        full_value,
        full_output,
        full_gate,
        full_up,
        full_down,
        full_gain_attn,
        full_gain_ffn,
        full_rel,
        full_lay,
    ) = weights
    normed_attn = rms_scale(tokens_f, full_gain_attn.astype(jnp.float32)).astype(jnp.bfloat16)
    queries = product(normed_attn, full_query).astype(jnp.bfloat16)
    keys_all = product(normed_attn, full_key).astype(jnp.bfloat16)
    values_all = product(normed_attn, full_value).astype(jnp.bfloat16)

    def forward_one_group(operands):
        query_group, key_group, value_group, table_group = operands
        scores = group_scores(query_group, key_group, table_group, onehot, valid)
        peak = jnp.max(scores, axis=-1, keepdims=True)
        expo = jnp.exp(scores - peak)
        total = jnp.sum(expo, axis=-1, keepdims=True)
        probs_low = (expo / total).astype(jnp.bfloat16)
        attended_group = jnp.einsum(
            "hij,jhd->ihd", probs_low, value_group, preferred_element_type=jnp.float32
        )
        return (attended_group.astype(jnp.bfloat16), (peak + jnp.log(total))[..., 0])

    stacked, log_totals = lax.map(
        forward_one_group,
        (
            split_heads(queries),
            split_heads(keys_all),
            split_heads(values_all),
            group_tables(table_pair(full_rel, full_lay)),
        ),
    )
    attended = join_heads(stacked)
    hidden_one = tokens_f + product(attended, full_output)
    normed_ffn = rms_scale(hidden_one, full_gain_ffn.astype(jnp.float32)).astype(jnp.bfloat16)
    gate_act = product(normed_ffn, full_gate)
    up_proj = product(normed_ffn, full_up)
    mixed = gated_product(gate_act, up_proj).astype(jnp.bfloat16)
    result = hidden_one + product(mixed, full_down)
    return (
        result,
        (
            normed_attn,
            queries,
            keys_all,
            values_all,
            log_totals,
            attended,
            hidden_one,
            normed_ffn,
            gate_act,
            up_proj,
            mixed,
        ),
    )


def attention_backward(
    queries, keys_all, values_all, log_totals, grad_attended, table_all, onehot, valid
):

    def attention_one_group(operands):
        query_group, key_group, value_group, table_group, lse_group, grad_group = operands
        scores = group_scores(query_group, key_group, table_group, onehot, valid)
        probs = jnp.exp(scores - lse_group[..., None])
        probs_low = probs.astype(jnp.bfloat16)
        grad_values = jnp.einsum(
            "hij,ihd->jhd", probs_low, grad_group, preferred_element_type=jnp.float32
        )
        grad_probs = jnp.einsum(
            "ihd,jhd->hij", grad_group, value_group, preferred_element_type=jnp.float32
        )
        grad_scores = (
            probs * (grad_probs - jnp.sum(probs * grad_probs, axis=-1, keepdims=True))
        ).astype(jnp.bfloat16)
        grad_queries = jnp.einsum(
            "hij,jhd->ihd", grad_scores, key_group, preferred_element_type=jnp.float32
        )
        grad_keys = jnp.einsum(
            "hij,ihd->jhd", grad_scores, query_group, preferred_element_type=jnp.float32
        )
        grad_table = jnp.einsum(
            "hij,ijb->bh", grad_scores, onehot, preferred_element_type=jnp.float32
        )
        return (
            grad_queries.astype(jnp.bfloat16),
            grad_keys.astype(jnp.bfloat16),
            grad_values.astype(jnp.bfloat16),
            grad_table,
        )

    grad_q_all, grad_k_all, grad_v_all, grad_tables = lax.map(
        attention_one_group,
        (
            split_heads(queries),
            split_heads(keys_all),
            split_heads(values_all),
            group_tables(table_all),
            log_totals,
            split_heads(grad_attended),
        ),
    )
    grad_table_all = jnp.moveaxis(grad_tables, 0, 1).reshape(2 * NB, H)
    return (join_heads(grad_q_all), join_heads(grad_k_all), join_heads(grad_v_all), grad_table_all)


MESH_ID = pl.DeviceIdType.MESH
BF = jnp.bfloat16
F32 = jnp.float32
X_BIT = 2
Y_BIT = 4
PARTS = ((X_BIT, Y_BIT), (Y_BIT, X_BIT))


class Links:
    def __init__(self, nn, send_sem, recv_sem):
        self.nn = nn
        self.w = lax.axis_index("wide")
        self.z = lax.axis_index("narrow")
        self.send_sem = send_sem
        self.recv_sem = recv_sem
        self.used = 0
        self.sent = []

    def fresh(self):
        self.used += 1
        return self.used - 1

    def wide(self, bit):
        return (jnp.bitwise_xor(self.w, bit), self.z)

    def along(self, step):
        return (self.w, lax.rem(self.z + step, self.nn))

    def copy(self, src, dst, number, device):
        return pltpu.make_async_remote_copy(
            src_ref=src,
            dst_ref=dst,
            send_sem=self.send_sem.at[number],
            recv_sem=self.recv_sem.at[number],
            device_id=device,
            device_id_type=MESH_ID,
        )

    def send(self, src, dst, number, device):
        copy = self.copy(src, dst, number, device)
        copy.start()
        self.sent.append(copy)

    def greet(self):
        barrier = pltpu.get_barrier_semaphore()
        others = [self.wide(bit) for bit in (1, X_BIT, Y_BIT)]
        others += [self.along(step) for step in range(1, self.nn)]
        for other in others:
            pl.semaphore_signal(barrier, inc=1, device_id=other, device_id_type=MESH_ID)
        pl.semaphore_wait(barrier, len(others))

    def finish(self):
        for copy in self.sent:
            copy.wait_send()


class Gather:
    def __init__(self, links, shard, full, rows, window, parts, local_sem, line=None, merged=None):
        self.links, self.shard, self.full, self.rows, self.parts = links, shard, full, rows, parts
        self.window = window
        self.local_sem, self.line, self.merged = local_sem, line, merged
        nn = links.nn
        self.block = rows * nn
        self.line_ids = [links.fresh() for _ in range(1, nn)]
        self.part_ids = {
            (p, mask): links.fresh()
            for p in range(len(parts))
            for mask in (X_BIT, Y_BIT, X_BIT | Y_BIT)
        }
        self.core_ids = {mask: links.fresh() for mask in (0, X_BIT, Y_BIT, X_BIT | Y_BIT)}

    def place(self, w, z):
        if self.line is not None:
            return self.line.at[z]
        return self.full.at[pl.ds((w * self.links.nn + z) * self.rows, self.rows), pl.ds(*self.window)]

    def span(self, mask, part=None):
        rows = pl.ds(jnp.bitwise_xor(self.links.w, mask) * self.block, self.block)
        low, size = self.window if part is None else self.parts[part][:2]
        return self.full.at[rows, pl.ds(low, size)]

    def own(self):
        return pltpu.make_async_copy(
            self.shard, self.place(self.links.w, self.links.z), self.local_sem
        )

    def start(self):
        k = self.links
        self.own().start()
        for step in range(1, k.nn):
            k.send(self.shard, self.place(k.w, k.z), self.line_ids[step - 1], k.along(step))

    def ready(self):
        k = self.links
        self.own().wait()
        for step in range(1, k.nn):
            came = lax.rem(k.z - step + k.nn, k.nn)
            k.copy(
                self.shard, self.place(k.w, came), self.line_ids[step - 1], k.along(step)
            ).wait_recv()
        if self.line is not None:
            whole = jnp.concatenate(
                [self.line[z, : self.rows].astype(F32) for z in range(k.nn)], axis=0
            )
            self.merged[...] = whole.astype(BF)
            move = pltpu.make_async_copy(self.merged, self.span(0), self.local_sem)
            move.start()
            move.wait()

    def spread(self):
        k = self.links
        for p, part in enumerate(self.parts):
            for bit in part[2]:
                k.send(self.span(0, p), self.span(0, p), self.part_ids[p, bit], k.wide(bit))
        k.send(self.span(0), self.span(0), self.core_ids[0], k.wide(1))

    def arrive(self, p, mask):
        k = self.links
        k.copy(
            self.span(mask, p), self.span(mask, p), self.part_ids[p, mask], k.wide(X_BIT)
        ).wait_recv()

    def forward(self):
        k = self.links
        for p, part in enumerate(self.parts):
            first, second = part[2]
            self.arrive(p, first)
            both = first | second
            k.send(self.span(first, p), self.span(first, p), self.part_ids[p, both], k.wide(second))

    def settle(self):
        k = self.links
        for p, part in enumerate(self.parts):
            self.arrive(p, part[2][1])
        for mask in (X_BIT, Y_BIT):
            k.send(self.span(mask), self.span(mask), self.core_ids[mask], k.wide(1))

    def last(self):
        k = self.links
        both = X_BIT | Y_BIT
        for p in range(len(self.parts)):
            self.arrive(p, both)
        k.send(self.span(both), self.span(both), self.core_ids[both], k.wide(1))

    def done(self):
        k = self.links
        for mask, number in self.core_ids.items():
            place = self.span(mask | 1)
            k.copy(place, place, number, k.wide(1)).wait_recv()


def halves(columns, first=0):
    low = columns // 256 * 128
    return ((first, low, PARTS[0]), (first + low, columns - low, PARTS[1]))


class GatherSquare:
    def __init__(self, links, shard, full, rows, window, local_sem, square, lines, merged):
        self.links, self.shard, self.full, self.rows, self.window = links, shard, full, rows, window
        self.square, self.lines, self.merged, self.local_sem = square, lines, merged, local_sem
        self.parts = halves(window[1])
        self.block = rows * links.nn
        self.part_ids = {
            (p, mask): links.fresh()
            for p in range(len(self.parts))
            for mask in (X_BIT, Y_BIT, X_BIT | Y_BIT)
        }
        self.line_ids = [links.fresh() for _ in range(1, links.nn)]
        self.core_ids = [links.fresh() for _ in range(square.shape[0])]

    def spot(self, mask, p):
        low, size = self.parts[p][:2]
        return self.square.at[jnp.bitwise_xor(self.links.w, mask) // 2, :, pl.ds(low, size)]

    def own(self):
        return pltpu.make_async_copy(
            self.shard, self.square.at[self.links.w // 2], self.local_sem.at[0]
        )

    def start(self):
        k = self.links
        self.own().start()
        for p, (low, size, order) in enumerate(self.parts):
            for bit in order:
                k.send(self.shard.at[:, pl.ds(low, size)], self.spot(0, p), self.part_ids[p, bit], k.wide(bit))

    def arrive(self, p, mask):
        k = self.links
        k.copy(self.spot(mask, p), self.spot(mask, p), self.part_ids[p, mask], k.wide(X_BIT)).wait_recv()

    def forward(self):
        k = self.links
        for p, (low, size, (first, second)) in enumerate(self.parts):
            self.arrive(p, first)
            k.send(self.spot(first, p), self.spot(first, p), self.part_ids[p, first | second], k.wide(second))
        for p, (low, size, (first, second)) in enumerate(self.parts):
            self.arrive(p, second)

    def keep(self):
        return pltpu.make_async_copy(self.square, self.lines.at[self.links.z], self.local_sem.at[0])

    def line(self):
        k = self.links
        self.own().wait()
        for p in range(len(self.parts)):
            self.arrive(p, X_BIT | Y_BIT)
        self.keep().start()
        for step in range(1, k.nn):
            k.send(self.square, self.lines.at[k.z], self.line_ids[step - 1], k.along(step))

    def rows_of(self, square, core):
        rows = pl.ds((square * 2 + core) * self.block, self.block)
        return self.full.at[rows, pl.ds(*self.window)]

    def out(self, square):
        core = lax.rem(self.links.w, 2)
        return pltpu.make_async_copy(
            self.merged.at[square], self.rows_of(square, core), self.local_sem.at[1 + square]
        )

    def join(self):
        k = self.links
        self.keep().wait()
        for step in range(1, k.nn):
            came = lax.rem(k.z - step + k.nn, k.nn)
            k.copy(self.square, self.lines.at[came], self.line_ids[step - 1], k.along(step)).wait_recv()

        def one(square, carry):
            whole = jnp.concatenate(
                [self.lines[z, square, : self.rows].astype(F32) for z in range(k.nn)], axis=0
            )
            self.merged[square] = whole.astype(BF)
            return carry

        lax.fori_loop(0, self.merged.shape[0], one, 0)
        core = lax.rem(k.w, 2)
        for square, number in enumerate(self.core_ids):
            self.out(square).start()
            k.send(self.merged.at[square], self.rows_of(square, core), number, k.wide(1))

    def done(self):
        k = self.links
        core = lax.rem(k.w, 2)
        for square, number in enumerate(self.core_ids):
            self.out(square).wait()
            k.copy(self.merged.at[square], self.rows_of(square, 1 - core), number, k.wide(1)).wait_recv()


def dot(left, right):
    return jnp.dot(left, right, preferred_element_type=F32)


def dot_nt(left, right):
    return lax.dot_general(left, right, (((1,), (1,)), ((), ())), preferred_element_type=F32)


def dot_tn(left, right):
    return lax.dot_general(left, right, (((0,), (0,)), ((), ())), preferred_element_type=F32)


def iota(shape, dimension):
    return lax.broadcasted_iota(jnp.int32, shape, dimension)


def ones_where(mask):
    return jnp.where(mask, 1.0, 0.0).astype(BF)


def unpack_row(rows, first, each, total):
    devices = rows.shape[0]
    pick = ones_where(iota((128, total), 0) == first + lax.rem(iota((128, total), 1), each))
    spread = dot(rows.astype(BF), pick)
    mine = iota((devices, total), 1) // each == iota((devices, total), 0)
    return jnp.sum(jnp.where(mine, spread, 0.0), axis=0, keepdims=True)


def table_block(rows, first):
    pick_shape = (H * QB, 128)
    total = None
    for index in range(2):
        lane = first + H * index + iota(pick_shape, 0) // QB
        pick = ones_where(iota(pick_shape, 1) == lane)
        table = dot_nt(pick, rows.astype(BF)).astype(BF)
        wide = (NB, QB * 2 * NB)
        spread = dot(table, ones_where(lax.rem(iota(wide, 1), 2 * NB) == iota(wide, 0) + NB * index))
        total = spread if total is None else total + spread
    shape = (H * QB, QB * 2 * NB)
    mine = lax.rem(iota(shape, 0), QB) == iota(shape, 1) // (2 * NB)
    return jnp.where(mine, total, 0.0).astype(BF)


def bucket_ones(rel, lay, onehot, block):
    width = rel.shape[1]
    rows = iota((NB, width), 0)
    for query in range(QB):
        for index, bucket in enumerate((rel, lay)):
            row = bucket[pl.ds(block * QB + query, 1), :]
            low = (query * 2 + index) * NB
            onehot[low : low + NB, :] = ones_where(jnp.broadcast_to(row, (NB, width)) == rows)


def forward_kernel(nn, shapes, *refs):
    count = len(shapes)
    occupied, tokens, rel_hbm, lay_hbm, cotangent = refs[:5]
    shards = refs[5 : 5 + count]
    refs = refs[5 + count :]
    fulls, refs = refs[:count], refs[count:]
    (grad_h, na_t, q_t, k_h, v_h, att_t, hid_h, nf_t, mix_h, probs_h, slope_h, act_h) = refs[:12]
    down_grads, down_came, refs = refs[12], refs[13], refs[14:]
    (
        line,
        merged,
        x,
        rel,
        lay,
        small,
        lhs,
        onehot,
        bias,
        na,
        q,
        k,
        v,
        att,
        hid,
        nf,
        mix,
        slope,
        act,
        probs,
        w_one,
        w_wide,
        grad,
        down_stage,
        gains,
        turned,
        mixed_t,
        send_sem,
        recv_sem,
        gather_sem,
        local_sem,
        ring_sem,
        rest_square,
        rest_lines,
        rest_merged,
        rest_sem,
    ) = refs
    slots, width = x.shape
    links = Links(nn, send_sem, recv_sem)
    numbers = iter(range(64))

    def move(src, dst):
        copy = pltpu.make_async_copy(src, dst, local_sem.at[next(numbers)])
        copy.start()
        return copy

    arriving = [move(tokens, x), move(rel_hbm, rel), move(lay_hbm, lay)]
    grad_in = move(cotangent, grad)
    links.greet()
    g = []
    first_up = UP_TILES * TILE
    cuts = [(0, columns) for rows, columns in shapes]
    cuts[6:] = [(0, first_up), (first_up, shapes[6][1] - first_up), (0, width - REST)]
    for number, (low, columns) in enumerate(cuts):
        index = min(number, 6) if number < 8 else 7
        rows = shapes[index][0]
        odd = index == 7
        g.append(
            Gather(
                links,
                shards[index].at[:, pl.ds(low, columns)],
                w_wide.at[index - 5] if index in (5, 6) else fulls[index],
                rows,
                (low, columns),
                halves(columns, low) if columns > 128 else ((0, columns, PARTS[0]),),
                gather_sem.at[number],
                line if odd else None,
                merged if odd else None,
            )
        )
    rows, columns = shapes[-1]
    rest = GatherSquare(
        links,
        shards[-1].at[:, pl.ds(columns - REST, REST)],
        fulls[-1],
        rows,
        (columns - REST, REST),
        rest_sem,
        rest_square,
        rest_lines,
        rest_merged,
    )
    down_id = links.used
    small_g, q_g, k_g, v_g, o_g, gate_g, up_g, up_two_g, down_g = g
    leaving = []
    turning = {}
    ffn = mixed_t.shape[0]
    tiles = ffn // TILE
    across = slots // TILE
    pairs = H // 2
    blocks = slots // QB
    block, piece = down_stage.shape[3:]
    chunks = width // piece
    squares = down_stage.shape[1]
    valid = iota((1, slots), 1) < occupied[0] + IMG

    def turn_out(slot, source, target):
        if slot in turning:
            turning[slot].wait()

        def one(tile, carry):
            at = pl.ds(pl.multiple_of(tile * TILE, TILE), TILE)
            turned[slot, at, :] = source[:, at].T
            return carry

        lax.fori_loop(0, width // TILE, one, 0)
        turning[slot] = move(turned.at[slot], target)

    def unpack():
        rows = small.reshape(small.shape[0] // 8, 8, 128)[:, 0, :]
        each = width // rows.shape[0]
        gains[0:1, :] = unpack_row(rows, 0, each, width)
        gains[1:2, :] = unpack_row(rows, each, each, width)
        lhs[...] = table_block(rows, 2 * each)

    def normalise(source, row, target):
        def one(index, carry):
            at = pl.ds(pl.multiple_of(index * 64, 64), 64)
            values = source[at, :].astype(F32)
            scale = lax.rsqrt(jnp.mean(values * values, axis=-1, keepdims=True) + RMS_EPSILON)
            target[at, :] = (values * scale * gains[row : row + 1, :]).astype(BF)
            return carry

        lax.fori_loop(0, slots // 64, one, 0)

    def bias_block(block, carry):
        bucket_ones(rel, lay, onehot, block)
        found = jnp.where(valid, dot(lhs[...], onehot[...]), MASK_SCORE)
        bias[:, pl.ds(pl.multiple_of(block * QB, QB), QB), :] = found.reshape(H, QB, slots)
        return carry

    def add_bias(part, parts):
        lax.fori_loop(part * blocks // parts, (part + 1) * blocks // parts, bias_block, 0)

    def project(slot, target):
        def one(tile, carry):
            at = pl.ds(pl.multiple_of(tile * WIDE, WIDE), WIDE)
            target[:, at] = dot(na[...], w_one[slot, :, at]).astype(BF)
            return carry

        lax.fori_loop(0, width // WIDE, one, 0)

    def probs_out(pair):
        turn = lax.rem(pair, 2)
        return pltpu.make_async_copy(probs.at[turn], probs_h.at[pl.ds(pair * 2, 2)], ring_sem.at[turn])

    def attend_pair(pair, carry):
        @pl.when(pair >= 2)
        def _():
            probs_out(pair - 2).wait()

        at = pl.ds(pl.multiple_of(pair * 128, 128), 128)
        low = iota((slots, 128), 1) < HD
        queries = q[:, at]
        keys = k[:, at]
        found = []
        for side in range(2):
            mine = jnp.where(low if side == 0 else jnp.logical_not(low), queries, 0)
            scores = dot_nt(mine, keys) + bias[pair * 2 + side]
            peak = jnp.max(scores, axis=-1, keepdims=True)
            expo = jnp.exp(scores - peak)
            total = jnp.sum(expo, axis=-1, keepdims=True)
            share = (expo * (1.0 / total)).astype(BF)
            probs[lax.rem(pair, 2), side] = share
            found.append(dot(share, v[:, at]))
        att[:, at] = jnp.where(low, found[0], found[1]).astype(BF)
        probs_out(pair).start()
        return carry

    def attend(first, last):
        lax.fori_loop(first, last, attend_pair, 0)

    def output():
        def one(tile, carry):
            at = pl.ds(pl.multiple_of(tile * WIDE, WIDE), WIDE)
            hid[:, at] = x[:, at].astype(F32) + dot(att[...], w_one[1, :, at])
            return carry

        lax.fori_loop(0, width // WIDE, one, 0)
        leaving.append(move(hid, hid_h))

    def keep_valid():
        valid_rows = iota((slots, 1), 0) < occupied[0] + IMG

        def one(tile, carry):
            at = pl.ds(pl.multiple_of(tile * TILE, TILE), TILE)
            grad[:, at] = jnp.where(valid_rows, grad[:, at].astype(F32), 0.0).astype(BF)
            return carry

        lax.fori_loop(0, width // TILE, one, 0)
        leaving.append(move(grad, grad_h))

    def gate_spot(tile, second):
        at = pl.ds(pl.multiple_of(lax.rem(tile, across) * TILE, TILE), TILE)
        return bias.at[tile // across + second * (-(-tiles // across)), :, at]

    def gate_tile(tile, carry):
        at = pl.ds(pl.multiple_of(tile * TILE, TILE), TILE)
        gate = dot(nf[...], w_wide[0, :, at])
        square = gate * gate
        inner = GELU_SCALE * gate * (1.0 + GELU_CUBE * square)
        bend = jnp.tanh(inner)
        half = 0.5 * (1.0 + bend)
        gate_spot(tile, 0)[...] = gate * half
        gate_spot(tile, 1)[...] = half + 0.5 * gate * (1.0 - bend * bend) * GELU_SCALE * (
            1.0 + 3.0 * GELU_CUBE * square
        )
        return carry

    def ffn_out(tile):
        turn = lax.rem(tile, 2)
        at = pl.ds(pl.multiple_of(tile * TILE, TILE), TILE)
        return (
            pltpu.make_async_copy(slope.at[turn], slope_h.at[:, at], ring_sem.at[2 + turn]),
            pltpu.make_async_copy(act.at[turn], act_h.at[:, at], ring_sem.at[4 + turn]),
            pltpu.make_async_copy(mix.at[turn], mix_h.at[:, at], ring_sem.at[6 + turn]),
        )

    def ffn_tile(tile, carry):
        @pl.when(tile >= 2)
        def _():
            for copy in ffn_out(tile - 2):
                copy.wait()

        at = pl.ds(pl.multiple_of(tile * TILE, TILE), TILE)
        turn = lax.rem(tile, 2)
        up = dot(nf[...], w_wide[1, :, at])
        active = gate_spot(tile, 0)[...]
        rise = gate_spot(tile, 1)[...]
        mixed = (active * up).astype(BF)
        mix[turn] = mixed
        mixed_t[at, :] = mixed.T
        act[turn] = active.astype(BF)
        slope[turn] = (up * rise).astype(BF)
        for copy in ffn_out(tile):
            copy.start()
        return carry

    def down_place(chunk, half):
        return down_grads.at[chunk, pl.ds(half * squares, squares)]

    def down_copy(unit):
        half, chunk, turn = unit // chunks, lax.rem(unit, chunks), lax.rem(unit, 2)
        return pltpu.make_async_copy(down_stage.at[turn], down_place(chunk, half), ring_sem.at[8 + turn])

    def down_trade(unit):
        half, chunk = unit // chunks, lax.rem(unit, chunks)
        core = lax.rem(links.w, 2)
        there = pl.ds(half * squares, squares)
        return links.copy(
            down_grads.at[chunk, there, 1 - core],
            down_came.at[chunk, there],
            down_id + unit,
            links.wide(1),
        )

    def down_unit(unit, carry):
        half, chunk = unit // chunks, lax.rem(unit, chunks)
        size = 2 * squares * block
        rows = pl.ds(pl.multiple_of(half * size, 16), size)
        at = pl.ds(pl.multiple_of(chunk * piece, piece), piece)
        found = dot(mixed_t[rows, :], grad[:, at])
        down_stage[lax.rem(unit, 2)] = found.astype(BF).reshape(down_stage.shape[1:])
        down_copy(unit).start()

        @pl.when(unit >= 1)
        def _():
            down_copy(unit - 1).wait()
            down_trade(unit - 1).start()

        return carry

    def down_units(first, last):
        lax.fori_loop(first, last, down_unit, 0)

    small_g.start()
    q_g.start()
    rest.start()
    small_g.ready()
    small_g.spread()
    k_g.start()
    q_g.ready()
    q_g.spread()
    v_g.start()
    small_g.forward()
    small_g.settle()
    small_g.last()
    small_g.done()
    small_in = move(fulls[0], small)
    rest.forward()
    for copy in arriving:
        copy.wait()
    k_g.ready()
    k_g.spread()
    o_g.start()
    gate_g.start()
    q_g.forward()
    small_in.wait()
    unpack()
    normalise(x, 0, na)
    turn_out(0, na, na_t)
    q_g.settle()
    add_bias(0, 4)
    v_g.ready()
    v_g.spread()
    k_g.forward()
    q_g.last()
    add_bias(1, 4)
    k_g.settle()
    o_g.ready()
    o_g.spread()
    up_g.start()
    v_g.forward()
    add_bias(2, 4)
    k_g.last()
    v_g.settle()
    q_g.done()
    fetch_q = move(fulls[1], w_one.at[0])
    add_bias(3, 4)
    gate_g.ready()
    gate_g.spread()
    up_two_g.start()
    o_g.forward()
    fetch_q.wait()
    project(0, q)
    turn_out(1, q, q_t)
    k_g.done()
    fetch_k = move(fulls[2], w_one.at[1])
    v_g.last()
    fetch_k.wait()
    project(1, k)
    leaving.append(move(k, k_h))
    v_g.done()
    fetch_v = move(fulls[3], w_one.at[0])
    o_g.settle()
    fetch_v.wait()
    project(0, v)
    leaving.append(move(v, v_h))
    attend(0, 3)
    up_g.ready()
    up_g.spread()
    down_g.start()
    o_g.last()
    gate_g.forward()
    o_g.done()
    fetch_o = move(fulls[4], w_one.at[1])
    attend(3, 6)
    gate_g.settle()
    rest.line()
    attend(6, pairs)
    turn_out(0, att, att_t)
    fetch_o.wait()
    output()
    normalise(hid, 1, nf)
    turn_out(1, nf, nf_t)
    up_g.forward()
    up_two_g.ready()
    up_two_g.spread()
    grad_in.wait()
    keep_valid()
    down_g.ready()
    up_g.settle()
    gate_g.last()
    gate_g.done()
    leaving.append(move(w_wide.at[0], fulls[5]))
    lax.fori_loop(0, tiles, gate_tile, 0)
    up_g.last()
    up_two_g.forward()
    down_g.spread()
    up_g.done()
    lax.fori_loop(0, UP_TILES, ffn_tile, 0)
    up_two_g.settle()
    down_units(0, chunks)
    up_two_g.last()
    down_g.forward()
    down_g.settle()
    up_two_g.done()
    leaving.append(move(w_wide.at[1], fulls[6]))
    lax.fori_loop(UP_TILES, tiles, ffn_tile, 0)
    down_g.last()
    rest.join()
    down_units(chunks, 2 * chunks)
    down_copy(jnp.int32(2 * chunks - 1)).wait()
    down_trade(jnp.int32(2 * chunks - 1)).start()
    down_g.done()
    rest.done()
    for unit in range(2 * chunks):
        down_trade(jnp.int32(unit)).wait()
    for copy in leaving + list(turning.values()):
        copy.wait()
    for pair in (pairs - 2, pairs - 1):
        probs_out(pair).wait()
    for tile in (tiles - 2, tiles - 1):
        for copy in ffn_out(tile):
            copy.wait()
    links.finish()


def forward_all(nw, nn, counts, tokens, rel, lay, cotangent, shards, odd_rows):
    devices = nw * nn
    shapes = []
    for index, shard in enumerate(shards):
        rows = odd_rows if index == len(shards) - 1 else shard.shape[0]
        shapes.append((rows, shard.shape[1]))
    slots, width = tokens.shape
    copies = (len(shards) + 2) * (nn - 1 + 6 + nw // 2) + 2 * (width // DOWN_PIECE)
    ffn = shapes[5][1]
    low = jax.ShapeDtypeStruct((slots, width), BF)
    wide = jax.ShapeDtypeStruct((slots, ffn), BF)
    full = jax.ShapeDtypeStruct((slots, width), F32)
    out_shape = [
        jax.ShapeDtypeStruct((rows * devices, columns), shard.dtype)
        for (rows, columns), shard in zip(shapes, shards)
    ]
    low_t = jax.ShapeDtypeStruct((width, slots), BF)
    out_shape += [low, low_t, low_t, low, low, low_t, full, low_t, wide]
    out_shape += [jax.ShapeDtypeStruct((H, slots, slots), BF), wide, wide]
    down = (nw // 2, 2, nn * odd_rows, DOWN_PIECE)
    out_shape += [jax.ShapeDtypeStruct((width // DOWN_PIECE,) + down, BF)]
    out_shape += [jax.ShapeDtypeStruct((width // DOWN_PIECE, nw // 2, nn * odd_rows, DOWN_PIECE), BF)]
    tile_rows = shards[-1].shape[0]
    half = (tile_rows, REST)
    hbm = pl.BlockSpec(memory_space=pl.ANY)
    page = pltpu.VMEM((slots, width), BF)
    return pl.pallas_call(
        functools.partial(forward_kernel, nn, shapes),
        out_shape=out_shape,
        in_specs=[pl.BlockSpec(memory_space=pltpu.SMEM)] + [hbm] * (4 + len(shards)),
        out_specs=[hbm] * len(out_shape),
        scratch_shapes=[
            pltpu.VMEM((nn, tile_rows, width - REST), BF),
            pltpu.VMEM((nn * odd_rows, width - REST), BF),
            page,
            pltpu.VMEM((slots, slots), jnp.int32),
            pltpu.VMEM((slots, slots), jnp.int32),
            pltpu.VMEM((devices * 8, 128), F32),
            pltpu.VMEM((H * QB, QB * 2 * NB), BF),
            pltpu.VMEM((QB * 2 * NB, slots), BF),
            pltpu.VMEM((H, slots, slots), F32),
            page,
            page,
            page,
            page,
            page,
            pltpu.VMEM((slots, width), F32),
            page,
            pltpu.VMEM((2, slots, TILE), BF),
            pltpu.VMEM((2, slots, TILE), BF),
            pltpu.VMEM((2, slots, TILE), BF),
            pltpu.VMEM((2, 2, slots, slots), BF),
            pltpu.VMEM((2, width, width), BF),
            pltpu.VMEM((2, width, ffn), BF),
            page,
            pltpu.VMEM((2, down[0] // 2) + down[1:], BF),
            pltpu.VMEM((8, width), F32),
            pltpu.VMEM((2, width, slots), BF),
            pltpu.VMEM((ffn, slots), BF),
            pltpu.SemaphoreType.DMA((copies,)),
            pltpu.SemaphoreType.DMA((copies,)),
            pltpu.SemaphoreType.DMA((len(shards) + 1,)),
            pltpu.SemaphoreType.DMA((64,)),
            pltpu.SemaphoreType.DMA((10,)),
            pltpu.VMEM((nw // 2,) + half, BF),
            pltpu.VMEM((nn, nw // 2) + half, BF),
            pltpu.VMEM((nw // 2, nn * odd_rows, half[1]), BF),
            pltpu.SemaphoreType.DMA((1 + nw // 2,)),
        ],
        compiler_params=pltpu.CompilerParams(
            collective_id=0, has_side_effects=True, vmem_limit_bytes=63 * 2**20
        ),
    )(counts, tokens, rel, lay, cotangent, *shards)


class Scatter:
    def __init__(self, links, chunks, rows, columns, grads, came, slots, base, traded=False, first=0):
        self.links, self.chunks, self.rows, self.columns = links, chunks, rows, columns
        self.grads, self.came = grads, came
        (self.held, self.other, self.round, self.out_line, self.in_line, self.load_sem) = slots
        self.base = base
        self.traded = traded
        self.first = first
        self.block = rows * links.nn
        self.parts = halves(columns)
        self.core = lax.rem(links.w, 2)
        self.ring = self.held.shape[0]
        self.line_ring = self.out_line.shape[0]

    def number(self, chunk, kind):
        return self.base + chunk * SCATTER_COPIES + kind

    def core_copy(self, chunk):
        return self.links.copy(
            self.grads.at[chunk, :, 1 - self.core],
            self.came.at[chunk],
            self.number(chunk, 0),
            self.links.wide(1),
        )

    def trade(self, chunk):
        self.core_copy(chunk).start()

    def loads(self, chunk):
        slot, turn = lax.rem(chunk, self.ring), lax.rem(chunk, 2)
        return (
            pltpu.make_async_copy(
                self.grads.at[chunk, :, self.core], self.held.at[slot], self.load_sem.at[turn, 0]
            ),
            pltpu.make_async_copy(
                self.came.at[chunk], self.other.at[turn], self.load_sem.at[turn, 1]
            ),
        )

    def fetch(self, chunk):
        if not self.traded:
            self.core_copy(chunk).wait_recv()
        for load in self.loads(chunk):
            load.start()

    def square(self, mask):
        return jnp.bitwise_xor(self.links.w, mask) // 2

    def hop(self, chunk, p, mask):
        slot = lax.rem(chunk, self.ring)
        low, size, order = self.parts[p]
        bit = order[1] if mask & order[1] else order[0]
        kind = 1 + p * 3 + (X_BIT, Y_BIT, X_BIT | Y_BIT).index(mask)
        return self.links.copy(
            self.held.at[slot, self.square(mask), :, pl.ds(low, size)],
            self.round.at[slot, kind - 1, :, pl.ds(0, size)],
            self.number(chunk, kind),
            self.links.wide(bit),
        )

    def landed(self, chunk, p, mask):
        return self.round.at[
            lax.rem(chunk, self.ring), p * 3 + (X_BIT, Y_BIT, X_BIT | Y_BIT).index(mask)
        ]

    def add_core(self, chunk):
        for load in self.loads(chunk):
            load.wait()
        slot, turn = lax.rem(chunk, self.ring), lax.rem(chunk, 2)

        def one(square, carry):
            self.held[slot, square] = (
                self.held[slot, square].astype(F32) + self.other[turn, square].astype(F32)
            ).astype(BF)
            return carry

        lax.fori_loop(0, self.held.shape[1], one, 0)
        for p, part in enumerate(self.parts):
            self.hop(chunk, p, X_BIT | Y_BIT).start()
        for p, part in enumerate(self.parts):
            self.hop(chunk, p, part[2][1]).start()

    def add_corner(self, chunk):
        slot = lax.rem(chunk, self.ring)
        for p, (low, size, order) in enumerate(self.parts):
            self.hop(chunk, p, X_BIT | Y_BIT).wait_recv()
            square = self.square(order[0])
            came = self.landed(chunk, p, X_BIT | Y_BIT)
            self.held[slot, square, :, low : low + size] = (
                self.held[slot, square, :, low : low + size].astype(F32)
                + came[:, :size].astype(F32)
            ).astype(BF)
        for p, part in enumerate(self.parts):
            self.hop(chunk, p, part[2][0]).start()

    def line_copy(self, chunk, step):
        k = self.links
        slot = lax.rem(chunk, self.line_ring)
        return k.copy(
            self.out_line.at[slot, lax.rem(k.z + step, k.nn)],
            self.in_line.at[slot, step - 1],
            self.number(chunk, 6 + step),
            k.along(step),
        )

    def add_square(self, chunk):
        slot, line = lax.rem(chunk, self.ring), lax.rem(chunk, self.line_ring)
        home = self.square(0)
        for p, (low, size, order) in enumerate(self.parts):
            total = self.held[slot, home, :, low : low + size].astype(F32)
            for mask in order:
                self.hop(chunk, p, mask).wait_recv()
                total = total + self.landed(chunk, p, mask)[:, :size].astype(F32)
            for z in range(self.links.nn):
                self.out_line[line, z, : self.rows, low : low + size] = total[
                    z * self.rows : (z + 1) * self.rows
                ].astype(BF)
        for step in range(1, self.links.nn):
            self.line_copy(chunk, step).start()
        if not self.traded:
            self.core_copy(chunk).wait_send()
        for p in range(len(self.parts)):
            for mask in (X_BIT, Y_BIT, X_BIT | Y_BIT):
                self.hop(chunk, p, mask).wait_send()

    def total(self, chunk):
        slot = lax.rem(chunk, self.line_ring)
        total = self.out_line[slot, self.links.z, : self.rows].astype(F32)
        for step in range(1, self.links.nn):
            self.line_copy(chunk, step).wait_recv()
            total = total + self.in_line[slot, step - 1, : self.rows].astype(F32)
        return total

    def pump(self, index, out):
        index = jnp.int32(index)
        steps = (self.fetch, self.add_core, self.add_corner, self.add_square, self.finish)
        for lag, action in zip(FEW_LAG if self.traded else LAG, steps):
            chunk = index - lag + self.first

            @pl.when(jnp.logical_and(chunk >= self.first, chunk < self.chunks))
            def _(chunk=chunk, action=action):
                action(chunk, out) if action == self.finish else action(chunk)

    def finish(self, chunk, out):
        out[chunk] = self.total(chunk)
        for step in range(1, self.links.nn):
            self.line_copy(chunk, step).wait_send()


class ScatterLine:
    def __init__(self, links, rows, columns, grads, came, slots, base):
        self.links, self.rows, self.columns = links, rows, columns
        self.grads, self.came = grads, came
        (self.held, self.other, self.square, self.round, self.in_line, self.load_sem) = slots
        self.base = base
        self.parts = halves(columns)
        self.core = lax.rem(links.w, 2)

    def number(self, chunk, kind):
        return self.base + chunk * SCATTER_COPIES + kind

    def core_copy(self, chunk):
        return self.links.copy(
            self.grads.at[chunk, :, 1 - self.core],
            self.came.at[chunk],
            self.number(chunk, 0),
            self.links.wide(1),
        )

    def loads(self, chunk):
        return (
            pltpu.make_async_copy(
                self.grads.at[chunk, :, self.core], self.held.at[chunk], self.load_sem.at[0]
            ),
            pltpu.make_async_copy(self.came.at[chunk], self.other, self.load_sem.at[1]),
        )

    def fetch(self, chunk):
        self.core_copy(chunk).wait_recv()
        for load in self.loads(chunk):
            load.start()

    def line_copy(self, chunk, step):
        k = self.links
        rows = pl.ds(pl.multiple_of(lax.rem(k.z + step, k.nn) * self.rows, self.rows), self.rows)
        return k.copy(
            self.held.at[chunk, :, rows],
            self.in_line.at[chunk, step - 1],
            self.number(chunk, 6 + step),
            k.along(step),
        )

    def add_core(self, chunk):
        for load in self.loads(chunk):
            load.wait()

        def one(square, carry):
            self.held[chunk, square] = (
                self.held[chunk, square].astype(F32) + self.other[square].astype(F32)
            ).astype(BF)
            return carry

        lax.fori_loop(0, self.held.shape[1], one, 0)
        for step in range(1, self.links.nn):
            self.line_copy(chunk, step).start()

    def spot(self, mask):
        return jnp.bitwise_xor(self.links.w, mask) // 2

    def hop(self, chunk, p, mask):
        low, size, order = self.parts[p]
        bit = order[1] if mask & order[1] else order[0]
        kind = 1 + p * 3 + (X_BIT, Y_BIT, X_BIT | Y_BIT).index(mask)
        return self.links.copy(
            self.square.at[chunk, self.spot(mask), :, pl.ds(low, size)],
            self.round.at[chunk, kind - 1],
            self.number(chunk, kind),
            self.links.wide(bit),
        )

    def landed(self, chunk, p, mask):
        kind = p * 3 + (X_BIT, Y_BIT, X_BIT | Y_BIT).index(mask)
        return self.round[chunk, kind].astype(F32)

    def add_line(self, chunk):
        for step in range(1, self.links.nn):
            self.line_copy(chunk, step).wait_recv()
        rows = pl.ds(pl.multiple_of(self.links.z * self.rows, self.rows), self.rows)
        for square in range(self.held.shape[1]):
            total = self.held[chunk, square, rows, :].astype(F32)
            for step in range(1, self.links.nn):
                total = total + self.in_line[chunk, step - 1, square].astype(F32)
            self.square[chunk, square] = total.astype(BF)
        for p, part in enumerate(self.parts):
            self.hop(chunk, p, X_BIT | Y_BIT).start()
        for p, part in enumerate(self.parts):
            self.hop(chunk, p, part[2][1]).start()

    def add_corner(self, chunk):
        for p, (low, size, order) in enumerate(self.parts):
            self.hop(chunk, p, X_BIT | Y_BIT).wait_recv()
            spot = self.spot(order[0])
            self.square[chunk, spot, :, low : low + size] = (
                self.square[chunk, spot, :, low : low + size].astype(F32)
                + self.landed(chunk, p, X_BIT | Y_BIT)
            ).astype(BF)
        for p, part in enumerate(self.parts):
            self.hop(chunk, p, part[2][0]).start()

    def finish(self, chunk, out):
        for p, (low, size, order) in enumerate(self.parts):
            total = self.square[chunk, self.spot(0), :, low : low + size].astype(F32)
            for mask in order:
                self.hop(chunk, p, mask).wait_recv()
                total = total + self.landed(chunk, p, mask)
            out[chunk, :, low : low + size] = total
        self.core_copy(chunk).wait_send()
        for step in range(1, self.links.nn):
            self.line_copy(chunk, step).wait_send()
        for p in range(len(self.parts)):
            for mask in (X_BIT, Y_BIT, X_BIT | Y_BIT):
                self.hop(chunk, p, mask).wait_send()


class ScatterSmall:
    def __init__(self, links, grads, out, came, round_in, line_in, mine):
        self.links, self.grads, self.out = links, grads, out
        self.came, self.round, self.line, self.mine = came, round_in, line_in, mine
        self.home = links.w // 2
        self.masks = (X_BIT, Y_BIT, X_BIT | Y_BIT)
        self.core_id = links.fresh()
        self.square_ids = [links.fresh() for _ in self.masks]
        self.line_ids = [links.fresh() for _ in range(1, links.nn)]

    def core_copy(self):
        k = self.links
        return k.copy(self.grads.at[:, 1 - lax.rem(k.w, 2)], self.came, self.core_id, k.wide(1))

    def square_copy(self, index):
        k, mask = self.links, self.masks[index]
        spot = jnp.bitwise_xor(k.w, mask) // 2
        return k.copy(self.mine.at[spot], self.round.at[index], self.square_ids[index], k.wide(mask))

    def line_copy(self, step):
        k = self.links
        rows = pl.ds(pl.multiple_of(lax.rem(k.z + step, k.nn) * 8, 8), 8)
        spot = self.mine.at[self.home, rows]
        return k.copy(spot, self.line.at[step - 1], self.line_ids[step - 1], k.along(step))

    def trade(self):
        self.core_copy().start()

    def spread(self):
        self.core_copy().wait()
        self.mine[...] = self.grads[:, lax.rem(self.links.w, 2)] + self.came[...]
        for index in range(len(self.masks)):
            self.square_copy(index).start()

    def along(self):
        for index in range(len(self.masks)):
            self.square_copy(index).wait()
        total = self.mine[self.home]
        for index in range(len(self.masks)):
            total = total + self.round[index]
        self.mine[self.home] = total
        for step in range(1, self.links.nn):
            self.line_copy(step).start()

    def finish(self):
        total = self.mine[self.home, pl.ds(pl.multiple_of(self.links.z * 8, 8), 8)]
        for step in range(1, self.links.nn):
            self.line_copy(step).wait()
            total = total + self.line[step - 1]
        self.out[...] = total


def padded(rows):
    return (rows + 15) // 16 * 16


def scatter_slots(squares, nn, rows, columns, ring, line_ring):
    half = columns // 2
    return [
        pltpu.VMEM((ring, squares, nn * rows, columns), BF),
        pltpu.VMEM((2, squares, nn * rows, columns), BF),
        pltpu.VMEM((ring, 6, nn * rows, half), BF),
        pltpu.VMEM((line_ring, nn, padded(rows), columns), BF),
        pltpu.VMEM((line_ring, nn - 1, padded(rows), columns), BF),
        pltpu.SemaphoreType.DMA((2, 2)),
    ]


def norm_pull(values, gain, grad):
    scale = lax.rsqrt(jnp.mean(values * values, axis=-1, keepdims=True) + RMS_EPSILON)
    scaled = grad * gain
    along = jnp.mean(scaled * values, axis=-1, keepdims=True)
    share = grad * values * scale
    return scale * scaled - values * (scale * scale * scale * along), share


def fold_rows(values):
    return jnp.sum(values.reshape(values.shape[0] // 8, 8, values.shape[1]), axis=0)


def pack_row(row, first, each, devices):
    total = row.shape[1]
    shape = (128, total)
    pick = jnp.where(iota(shape, 0) == first + lax.rem(iota(shape, 1), each), 1.0, 0.0)
    shape = (devices, total)
    mine = jnp.where(iota(shape, 1) // each == iota(shape, 0), row, 0.0)
    return lax.dot_general(
        mine,
        pick,
        (((1,), (1,)), ((), ())),
        preferred_element_type=F32,
        precision=lax.Precision.HIGHEST,
    )


def backward_kernel(nn, few_facts, many_facts, *refs):
    occupied, refs = refs[0], refs[1:]
    (
        tokens,
        rel_hbm,
        lay_hbm,
        grad_h,
        small_h,
        query_h,
        key_h,
        value_h,
        output_h,
        gate_h,
        up_h,
        down_h,
        na_t,
        q_t,
        k_h,
        v_h,
        att_t,
        hid_h,
        nf_t,
        mix_h,
        probs_h,
        slope_h,
        act_h,
        few_grads,
        few_came,
    ) = refs[:25]
    refs = refs[25:]
    (out_h, rows_out, few_out, many_out, small_out, many_grads, many_came) = refs[:7]
    few_slots, many_slots, late_slots, refs = refs[7:13], refs[13:19], refs[19:25], refs[25:]
    (
        x,
        rel,
        lay,
        small,
        gains,
        grad,
        left,
        acc,
        hid,
        wd_s,
        wgu_s,
        pair,
        slope_s,
        act_s,
        many_stage,
        branch,
        w_one,
        pull,
        pull_t,
        qt,
        k,
        v,
        probs,
        pieces,
        onehot,
        table,
        sums,
        small_grads,
        small_came,
        small_round,
        small_line,
        small_mine,
        send_sem,
        recv_sem,
        local_sem,
        tile_sem,
        stage_sem,
        probs_sem,
    ) = refs
    slots, width = x.shape
    links = Links(nn, send_sem, recv_sem)
    numbers = iter(range(64))

    def later_move(src, dst):
        return pltpu.make_async_copy(src, dst, local_sem.at[next(numbers)])

    def move(src, dst):
        copy = later_move(src, dst)
        copy.start()
        return copy

    few = Scatter(links, *few_facts, few_grads, few_came, few_slots, 0, traded=True)
    base = few_facts[0] * SCATTER_COPIES
    many = Scatter(links, *many_facts, many_grads, many_came, many_slots, base, first=LATE)
    late = ScatterLine(links, *many_facts[1:], many_grads, many_came, late_slots, base)
    links.used = base + many_facts[0] * SCATTER_COPIES
    little = ScatterSmall(
        links, small_grads, small_out, small_came, small_round, small_line, small_mine
    )
    ffn = mix_h.shape[1]
    tiles = ffn // TILE
    pairs = H // 2
    wide = many.columns
    squares = many_stage.shape[1]
    devices = small.shape[0] // 8
    each = width // devices
    zero = jnp.zeros((8, width), F32)

    def tile_copies(tile):
        turn = lax.rem(tile, 2)
        at = pl.ds(pl.multiple_of(tile * TILE, TILE), TILE)
        return [
            pltpu.make_async_copy(src, dst, tile_sem.at[turn, index])
            for index, (src, dst) in enumerate(
                (
                    (down_h.at[at], wd_s.at[turn]),
                    (gate_h.at[:, at], wgu_s.at[turn, :, pl.ds(0, TILE)]),
                    (up_h.at[:, at], wgu_s.at[turn, :, pl.ds(TILE, TILE)]),
                    (slope_h.at[:, at], slope_s.at[turn]),
                    (act_h.at[:, at], act_s.at[turn]),
                )
            )
        ]

    def many_copy(chunk):
        turn = lax.rem(chunk, 2)
        return pltpu.make_async_copy(many_stage.at[turn], many.grads.at[chunk], stage_sem.at[turn])

    def flush(chunk):
        many_copy(chunk).wait()
        many.trade(chunk)

    def make(chunk, left_rows, right, dot_one):
        found = dot_one(left_rows[...], right())
        many_stage[lax.rem(chunk, 2)] = found.astype(BF).reshape(many_stage.shape[1:])
        many_copy(chunk).start()

    def few_pump(index):
        few.pump(index, few_out)

    def many_pump(index):
        many.pump(index, many_out)

    def ffn_tile(tile, carry):
        turn = lax.rem(tile, 2)

        @pl.when(tile + 1 < tiles)
        def _():
            for copy in tile_copies(tile + 1):
                copy.start()

        @pl.when(tile == 3)
        def _():
            start(*later)
            start(*last)

        for copy in tile_copies(tile):
            copy.wait()
        grad_mixed = dot_nt(grad[...], wd_s[turn])
        pair[:, :TILE] = (grad_mixed * slope_s[turn].astype(F32)).astype(BF)
        pair[:, TILE:] = (grad_mixed * act_s[turn].astype(F32)).astype(BF)
        make(tile, left, lambda: pair[...], dot)

        @pl.when(lax.rem(tile, 2) == 1)
        def _():
            few_pump(tile // 2 + 2)

        acc[...] += dot_nt(pair[...], wgu_s[turn])
        flush(tile)
        many_pump(tile - FFN_LAG)

        @pl.when(jnp.logical_and(tile >= 2, tile < 2 + LATE))
        def _():
            late.add_core(tile - 2)

        @pl.when(jnp.logical_and(tile >= 1, tile < 1 + LATE))
        def _():
            late.fetch(tile - 1)

        return carry

    def unpack():
        rows = small.reshape(devices, 8, 128)[:, 0, :]
        gains[0:1, :] = unpack_row(rows, 0, each, width)
        gains[1:2, :] = unpack_row(rows, each, each, width)

    def norm_two():
        def one(index, total):
            at = pl.ds(pl.multiple_of(index * 64, 64), 64)
            part, share = norm_pull(hid[at, :], gains[1:2, :], acc[at, :])
            whole = grad[at, :].astype(F32) + part
            hid[at, :] = whole
            branch[at, :] = whole.astype(BF)
            return total + fold_rows(share)

        sums[0] = lax.fori_loop(0, slots // 64, one, zero)

    def output_chunk(part, carry):
        at = pl.ds(pl.multiple_of(part * wide, wide), wide)
        make(tiles + part, pull_t, lambda: branch[:, at], dot)
        return carry

    def pull_back():
        def one(tile, carry):
            at = pl.ds(pl.multiple_of(tile * WIDE, WIDE), WIDE)
            found = dot_nt(branch[...], w_one[0, at, :]).astype(BF)
            pull[:, at] = found
            pull_t[at, :] = found.T
            return carry

        lax.fori_loop(0, width // WIDE, one, 0)

    def probs_copy(index):
        turn = lax.rem(index, 2)
        return pltpu.make_async_copy(
            probs_h.at[pl.ds(index * 2, 2)], probs.at[turn], probs_sem.at[turn]
        )

    def attend_pair(index, carry):
        @pl.when(index + 1 < pairs)
        def _():
            probs_copy(index + 1).start()

        probs_copy(index).wait()
        turn = lax.rem(index, 2)
        at = pl.ds(pl.multiple_of(index * 128, 128), 128)
        low = iota((slots, 128), 1) < HD
        keys, pulls, values = k[:, at], pull[:, at], v[:, at]
        found = []
        for side in range(2):
            head = index * 2 + side
            mine = jnp.where(low if side == 0 else jnp.logical_not(low), pulls, 0)
            share = probs[turn, side]
            wanted = dot_nt(mine, values)
            share_f = share.astype(F32)
            joint = share_f * wanted
            piece = (joint - share_f * jnp.sum(joint, axis=-1, keepdims=True)).astype(BF)
            pieces[pl.ds(pl.multiple_of(head * slots, slots), slots), :] = piece
            found.append(dot(piece, keys))
            rows = pl.ds(pl.multiple_of(head * HD, HD), HD)
            qt[rows, :] = dot(qt[rows, :], piece).astype(BF)
            pull_t[rows, :] = dot(pull_t[rows, :], share).astype(BF)
        pull[:, at] = jnp.where(low, found[0], found[1]).astype(BF)
        return carry

    def attend(first, last):
        lax.fori_loop(first, last, attend_pair, 0)

    first_head_chunk = tiles + width // wide

    def head_chunks(half):
        at = pl.ds(pl.multiple_of(half * wide, wide), wide)
        chunk = first_head_chunk + half * 3

        def turned_chunk(index, carry):
            found = jnp.where(index == 0, pull_t[at, :], qt[at, :])
            make(chunk + 2 * index, left, lambda: found, dot_nt)

            @pl.when(index == 0)
            def _():
                make(chunk + 1, left, lambda: pull[:, at], dot)
                flush(chunk)

            return carry

        lax.fori_loop(0, 2, turned_chunk, 0)
        flush(chunk + 1)
        flush(chunk + 2)

    def table_blocks(index, carry):
        sides = []
        for side in range(2):
            block = index * 2 + side
            at = slice(side * slots, (side + 1) * slots)
            for query in range(BACK_QB):
                for which, bucket in enumerate((rel, lay)):
                    row = bucket[pl.ds(block * BACK_QB + query, 1), :]
                    first = (query * 2 + which) * NB
                    onehot[first : first + NB, at] = ones_where(
                        jnp.broadcast_to(row, (NB, slots)) == iota((NB, slots), 0)
                    )
            heads = [
                pieces[pl.ds(pl.multiple_of(head * slots + block * BACK_QB, BACK_QB), BACK_QB), :]
                for head in range(H)
            ]
            sides.append(jnp.concatenate(heads, axis=0))
        table[...] += dot_nt(onehot[...], jnp.concatenate(sides, axis=1))
        return carry

    def add_table(part, parts):
        blocks = slots // BACK_QB // 2
        lax.fori_loop(part * blocks // parts, (part + 1) * blocks // parts, table_blocks, 0)

    whole = ffn // slots
    first_mix = width // slots * ffn

    def output_moves():
        moves = [
            later_move(down_h.at[:, pl.ds(part * slots, slots)], pieces.at[pl.ds(part * ffn, ffn)])
            for part in range(width // slots)
        ]
        moves += [
            later_move(
                mix_h.at[:, pl.ds(part * slots, slots)],
                pieces.at[pl.ds(first_mix + part * slots, slots)],
            )
            for part in range(whole)
        ]
        return moves + [later_move(mix_h.at[:, pl.ds(whole * slots, TILE)], slope_s.at[0])]

    def down_project(part):
        at = pl.ds(pl.multiple_of(part * slots, slots), slots)

        def one(index, total):
            rows = pl.ds(pl.multiple_of(part * ffn + index * slots, TILE), slots)
            mixed = pl.ds(pl.multiple_of(first_mix + index * slots, TILE), slots)
            acc[:, at] += dot(pieces[mixed, :], pieces[rows, :])
            return total

        lax.fori_loop(0, whole, one, 0)
        rows = pl.ds(pl.multiple_of(part * ffn + whole * slots, TILE), TILE)
        total = acc[:, at] + dot(slope_s[0], pieces[rows, :])
        valid_rows = iota((slots, 1), 0) < occupied[0] + IMG
        x[:, at] = jnp.where(valid_rows, total, 0.0).astype(BF)

    def turn_back():
        def one(tile, carry):
            at = pl.ds(pl.multiple_of(tile * TILE, TILE), TILE)
            v[:, at] = pull_t[at, :].T
            branch[:, at] = qt[at, :].T
            return carry

        lax.fori_loop(0, width // TILE, one, 0)

    def pull_normed(source, slot, first):
        def one(tile, carry):
            at = pl.ds(pl.multiple_of(tile * WIDE, WIDE), WIDE)
            found = dot_nt(source[...], w_one[slot, at, :])
            acc[:, at] = found if first else acc[:, at] + found
            return carry

        lax.fori_loop(0, width // WIDE, one, 0)

    def norm_one():
        def one(index, total):
            at = pl.ds(pl.multiple_of(index * 64, 64), 64)
            part, share = norm_pull(x[at, :].astype(F32), gains[0:1, :], acc[at, :])
            hid[at, :] += part
            return total + fold_rows(share)

        sums[1] = lax.fori_loop(0, slots // 64, one, zero)

    def pack():
        total = table[...]
        mine = iota(total.shape, 0) // (2 * NB) == lax.rem(iota(total.shape, 1), BACK_QB)
        folded = jnp.sum(
            jnp.where(mine, total, 0.0).reshape(BACK_QB, 2 * NB, H * BACK_QB), axis=0
        )
        packed = [
            pack_row(jnp.sum(sums[1], axis=0, keepdims=True), 0, each, devices),
            pack_row(jnp.sum(sums[0], axis=0, keepdims=True), 0, each, devices),
        ]
        shape = (H * BACK_QB, 128)
        pick = jnp.where(iota(shape, 1) == iota(shape, 0) // BACK_QB, 1.0, 0.0)
        for index in range(2):
            packed.append(
                jnp.dot(
                    folded[index * NB : (index + 1) * NB],
                    pick,
                    preferred_element_type=F32,
                    precision=lax.Precision.HIGHEST,
                )
            )
        small_grads[...] = jnp.zeros_like(small_grads)
        for device in range(devices):
            wide_at, z = divmod(device, nn)
            for index, rows in enumerate(packed):
                at = z * 8 + index
                small_grads[wide_at // 2, wide_at % 2, at : at + 1, :] = rows[device : device + 1]

    later = [
        later_move(*pair_of)
        for pair_of in (
            (hid_h, hid),
            (small_h, small),
            (att_t, pull_t),
            (output_h, w_one.at[0]),
            (q_t, qt),
            (k_h, k),
            (v_h, v),
        )
    ]
    last = [
        later_move(*pair_of)
        for pair_of in ((tokens, x), (rel_hbm, rel), (lay_hbm, lay), (value_h, w_one.at[1]))
    ]
    na_in, query_in, key_in = (
        later_move(*pair_of)
        for pair_of in ((na_t, left), (query_h, w_one.at[0]), (key_h, w_one.at[0]))
    )
    rows_copy, out_copy = later_move(hid, rows_out), later_move(x, out_h)
    output_in = output_moves()
    hid_in = later_move(hid_h, acc)

    def start(*copies):
        for copy in copies:
            copy.start()

    def wait(*copies):
        for copy in copies:
            copy.wait()

    few.fetch(jnp.int32(0))
    start(*tile_copies(0))
    first_in = [move(grad_h, grad), move(nf_t, left)]
    links.greet()
    few.fetch(jnp.int32(1))
    few.add_core(jnp.int32(0))
    acc[...] = jnp.zeros_like(acc)
    table[...] = jnp.zeros_like(table)
    wait(*first_in)
    lax.fori_loop(0, tiles, ffn_tile, 0)
    wait(*later)
    na_in.start()
    unpack()
    norm_two()
    def step(index, carry):
        few_pump(index + tiles // 2 + 2)
        many_pump(index + tiles - FFN_LAG)

        for lag, action in ((1, late.add_line), (3, late.add_corner), (5, late.finish)):
            chunk = index - lag

            @pl.when(jnp.logical_and(chunk >= 0, chunk < LATE))
            def _(chunk=chunk, action=action):
                action(chunk, many_out) if action == late.finish else action(chunk)

        @pl.when(index == 0)
        def _():
            lax.fori_loop(0, width // wide, output_chunk, 0)
            pull_back()
            flush(tiles)
            flush(tiles + 1)
            query_in.start()
            probs_copy(jnp.int32(0)).start()

        second = index >= 4
        turn = jnp.where(second, index - 4, index - 1)
        attends = jnp.logical_and(turn >= 0, turn < 2)

        @pl.when(attends)
        def _():
            first = 2 * turn + jnp.where(second, 4, 0)
            attend(first, first + 2)

        @pl.when(index == 3)
        def _():
            wait(*last)
            na_in.wait()

        @pl.when(jnp.logical_or(index == 3, index == 6))
        def _():
            head_chunks(index // 3 - 1)

        @pl.when(jnp.logical_and(index >= 7, index < 10))
        def _():
            add_table(index - 7, 3)

        @pl.when(index == 10)
        def _():
            start(*output_in)
            query_in.wait()
            turn_back()
            pull_normed(pull, 0, True)
            key_in.start()

        @pl.when(index == 11)
        def _():
            pull_normed(v, 1, False)
            key_in.wait()
            pull_normed(branch, 0, False)

        @pl.when(index == 12)
        def _():
            norm_one()
            rows_copy.start()
            hid_in.start()
            pack()
            little.trade()

        @pl.when(index == 13)
        def _():
            wait(*output_in)
            hid_in.wait()
            little.spread()

        @pl.when(index == 15)
        def _():
            little.along()

        @pl.when(jnp.logical_or(index == 14, index == 16))
        def _():
            down_project(index // 2 - 7)

        @pl.when(index == 17)
        def _():
            out_copy.start()

        return carry

    lax.fori_loop(0, many.chunks - LATE + LAGS - (tiles - FFN_LAG) + 1, step, 0)
    little.finish()
    wait(rows_copy, out_copy)
    links.finish()


def backward_all(nw, nn, counts, page, weights, saved):
    squares = nw // 2
    devices = nw * nn
    slots, width = page[0].shape
    ffn = weights[5].shape[1]
    few = (width // DOWN_PIECE, ffn // devices, DOWN_PIECE)
    many = (ffn // TILE + 8, width // devices, 2 * TILE)
    outs = [jax.ShapeDtypeStruct((slots, width), BF), jax.ShapeDtypeStruct((slots, width), F32)]
    for chunks, rows, columns in (few, many):
        outs.append(jax.ShapeDtypeStruct((chunks, rows, columns), F32))
    outs.append(jax.ShapeDtypeStruct((8, 128), F32))
    chunks, rows, columns = many
    outs.append(jax.ShapeDtypeStruct((chunks, squares, 2, nn * rows, columns), BF))
    outs.append(jax.ShapeDtypeStruct((chunks, squares, nn * rows, columns), BF))
    copies = (few[0] + many[0]) * SCATTER_COPIES + 16
    vmem = pl.BlockSpec(memory_space=pltpu.VMEM)
    hbm = pl.BlockSpec(memory_space=pl.ANY)
    low = pltpu.VMEM((slots, width), BF)
    turned = pltpu.VMEM((width, slots), BF)
    full = pltpu.VMEM((slots, width), F32)
    inputs = (counts,) + tuple(page) + tuple(weights) + tuple(saved)
    return pl.pallas_call(
        functools.partial(backward_kernel, nn, few, many),
        out_shape=outs,
        in_specs=[pl.BlockSpec(memory_space=pltpu.SMEM)] + [hbm] * (len(inputs) - 1),
        out_specs=[hbm, hbm, vmem, vmem, vmem, hbm, hbm],
        scratch_shapes=scatter_slots(squares, nn, few[1], few[2], few[0], few[0])
        + scatter_slots(squares, nn, many[1], many[2], RING, LINE_RING)
        + [
            pltpu.VMEM((LATE, squares, nn * many[1], many[2]), BF),
            pltpu.VMEM((squares, nn * many[1], many[2]), BF),
            pltpu.VMEM((LATE, squares, many[1], many[2]), BF),
            pltpu.VMEM((LATE, 6, many[1], many[2] // 2), BF),
            pltpu.VMEM((LATE, nn - 1, squares, many[1], many[2]), BF),
            pltpu.SemaphoreType.DMA((2,)),
        ]
        + [
            low,
            pltpu.VMEM((slots, slots), jnp.int32),
            pltpu.VMEM((slots, slots), jnp.int32),
            pltpu.VMEM((devices * 8, 128), F32),
            pltpu.VMEM((8, width), F32),
            low,
            turned,
            full,
            full,
            pltpu.VMEM((2, TILE, width), BF),
            pltpu.VMEM((2, width, 2 * TILE), BF),
            pltpu.VMEM((slots, 2 * TILE), BF),
            pltpu.VMEM((2, slots, TILE), BF),
            pltpu.VMEM((2, slots, TILE), BF),
            pltpu.VMEM((2, squares, 2, nn * many[1], many[2]), BF),
            low,
            pltpu.VMEM((2, width, width), BF),
            low,
            turned,
            turned,
            low,
            low,
            pltpu.VMEM((2, 2, slots, slots), BF),
            pltpu.VMEM((H * slots, slots), BF),
            pltpu.VMEM((BACK_QB * 2 * NB, 2 * slots), BF),
            pltpu.VMEM((BACK_QB * 2 * NB, H * BACK_QB), F32),
            pltpu.VMEM((2, 8, width), F32),
            pltpu.VMEM((squares, 2, nn * 8, 128), F32),
            pltpu.VMEM((squares, nn * 8, 128), F32),
            pltpu.VMEM((3, nn * 8, 128), F32),
            pltpu.VMEM((nn - 1, 8, 128), F32),
            pltpu.VMEM((squares, nn * 8, 128), F32),
            pltpu.SemaphoreType.DMA((copies,)),
            pltpu.SemaphoreType.DMA((copies,)),
            pltpu.SemaphoreType.DMA((64,)),
            pltpu.SemaphoreType.DMA((2, 5)),
            pltpu.SemaphoreType.DMA((2,)),
            pltpu.SemaphoreType.DMA((2,)),
        ],
        compiler_params=pltpu.CompilerParams(
            collective_id=1, has_side_effects=True, vmem_limit_bytes=63 * 2**20
        ),
    )(*inputs)[:5]


def place_kernel(few_h, many_h, rows_h, out_h, small, *refs):
    (whole_out, row_out, query, key, value, output, gate, up, down) = refs[:9]
    (gain_attn, gain_ffn, rel, lay) = refs[9:13]
    few, many, rows, whole, in_sem, out_sem = refs[13:]
    tiles = gate.shape[1] // TILE
    wide = many.shape[2]
    part = rows.shape[0] // 8
    arriving = [
        pltpu.make_async_copy(src, dst, in_sem.at[index])
        for index, (src, dst) in enumerate(
            [(many_h, many), (few_h, few), (out_h, whole)]
            + [
                (rows_h.at[pl.ds(index * part, part)], rows.at[pl.ds(index * part, part)])
                for index in range(8)
            ]
        )
    ]
    for copy in arriving:
        copy.start()
    moves = []

    def move(src, dst):
        copy = pltpu.make_async_copy(src, dst, out_sem.at[len(moves)])
        copy.start()
        moves.append(copy)

    for index, target in enumerate((gain_attn, gain_ffn, rel, lay)):
        target[...] = small[index, : target.shape[0]]
    arriving[0].wait()
    for tile in range(tiles):
        at = pl.ds(tile * TILE, TILE)
        move(many.at[tile, :, pl.ds(0, TILE)], gate.at[:, at])
        move(many.at[tile, :, pl.ds(TILE, TILE)], up.at[:, at])
    halves_of = output.shape[1] // wide
    for half in range(halves_of):
        at = pl.ds(half * wide, wide)
        move(many.at[tiles + half], output.at[:, at])
        first = tiles + halves_of + half * 3
        for index, target in enumerate((value, query, key)):
            move(many.at[first + index], target.at[:, at])
    arriving[1].wait()
    for chunk in range(few.shape[0]):
        move(few.at[chunk], down.at[:, pl.ds(chunk * few.shape[2], few.shape[2])])
    arriving[2].wait()
    move(whole, whole_out)
    for index in range(8):
        arriving[3 + index].wait()
        at = pl.ds(index * part, part)
        move(rows.at[at], row_out.at[at])
    for copy in moves:
        copy.wait()


def place_all(few, many, rows, out, small, shapes):
    hbm = pl.BlockSpec(memory_space=pl.ANY)
    vmem = pl.BlockSpec(memory_space=pltpu.VMEM)
    outs = [jax.ShapeDtypeStruct(out.shape, BF), jax.ShapeDtypeStruct(rows.shape, F32)]
    outs += [jax.ShapeDtypeStruct(shape, F32) for shape in shapes]
    return pl.pallas_call(
        place_kernel,
        out_shape=outs,
        in_specs=[hbm] * 4 + [vmem],
        out_specs=[hbm] * 9 + [vmem] * 4,
        scratch_shapes=[
            pltpu.VMEM(few.shape, F32),
            pltpu.VMEM(many.shape, F32),
            pltpu.VMEM(rows.shape, F32),
            pltpu.VMEM(out.shape, BF),
            pltpu.SemaphoreType.DMA((16,)),
            pltpu.SemaphoreType.DMA((64,)),
        ],
        compiler_params=pltpu.CompilerParams(vmem_limit_bytes=63 * 2**20),
    )(few, many, rows, out, small)


def local_fast(
    nw,
    nn,
    tokens,
    w_query,
    w_key,
    w_value,
    w_output,
    w_gate,
    w_up,
    w_down,
    gain_attn,
    gain_ffn,
    rel_table,
    lay_table,
    ocr_counts,
    rel_bucket,
    lay_bucket,
    cotangent,
):
    small = jnp.concatenate([gain_attn, gain_ffn, rel_table, lay_table]).astype(F32)
    small = jnp.pad(small[None], ((0, 7), (0, 128 - small.shape[0])))
    down = jnp.pad(w_down, ((0, padded(w_down.shape[0]) - w_down.shape[0]), (0, 0)))
    page = (tokens, rel_bucket, lay_bucket)
    shards = [small, w_query, w_key, w_value, w_output, w_gate, w_up, down]
    found = forward_all(nw, nn, ocr_counts, *page, cotangent, shards, w_down.shape[0])
    weights, grad, saved = found[: len(shards)], found[len(shards)], found[len(shards) + 1 :]
    output, grad_tokens, few, many, small = backward_all(
        nw, nn, ocr_counts, page + (grad,), weights, saved
    )

    square = w_query.shape
    shapes = [square] * 4 + [w_gate.shape, w_up.shape, w_down.shape]
    shapes += [part.shape for part in (gain_attn, gain_ffn, rel_table, lay_table)]
    return tuple(place_all(few, many, grad_tokens, output, small, shapes))


def local(
    tokens,
    w_query,
    w_key,
    w_value,
    w_output,
    w_gate,
    w_up,
    w_down,
    gain_attn,
    gain_ffn,
    rel_table,
    lay_table,
    ocr_counts,
    rel_bucket,
    lay_bucket,
    cotangent,
):
    slot = tokens.shape[0]
    valid = jnp.arange(slot) < ocr_counts[0] + IMG
    buckets = jnp.arange(NB)
    onehot = jnp.concatenate(
        [
            (rel_bucket[:, :, None] == buckets).astype(jnp.bfloat16),
            (lay_bucket[:, :, None] == buckets).astype(jnp.bfloat16),
        ],
        axis=2,
    )
    tokens_f = tokens.astype(jnp.float32)
    weights = gather_weights(
        w_query,
        w_key,
        w_value,
        w_output,
        w_gate,
        w_up,
        w_down,
        gain_attn,
        gain_ffn,
        rel_table,
        lay_table,
    )
    result, saved = forward_pass(tokens_f, weights, onehot, valid)
    output = jnp.where(valid[:, None], result, 0.0).astype(jnp.bfloat16)
    (
        full_query,
        full_key,
        full_value,
        full_output,
        full_gate,
        full_up,
        full_down,
        full_gain_attn,
        full_gain_ffn,
        full_rel,
        full_lay,
    ) = weights
    (
        normed_attn,
        queries,
        keys_all,
        values_all,
        log_totals,
        attended,
        hidden_one,
        normed_ffn,
        gate_act,
        up_proj,
        mixed,
    ) = saved
    grad_result = jnp.where(valid[:, None], cotangent.astype(jnp.float32), 0.0)
    grad_low = grad_result.astype(jnp.bfloat16)
    grad_down = contract_rows(mixed, grad_low)
    grad_mixed = contract_cols(grad_low, full_down)
    gated_value, gated_pull = jax.vjp(gated_product, gate_act, up_proj)
    grad_gate_act, grad_up_proj = gated_pull(grad_mixed)
    gate_low = grad_gate_act.astype(jnp.bfloat16)
    up_low = grad_up_proj.astype(jnp.bfloat16)
    grad_gate = contract_rows(normed_ffn, gate_low)
    grad_up = contract_rows(normed_ffn, up_low)
    grad_normed_ffn = contract_cols(gate_low, full_gate) + contract_cols(up_low, full_up)
    norm_value, norm_pull = jax.vjp(rms_scale, hidden_one, full_gain_ffn.astype(jnp.float32))
    grad_hidden_part, grad_gain_ffn = norm_pull(grad_normed_ffn)
    grad_hidden = grad_result + grad_hidden_part
    branch_low = grad_hidden.astype(jnp.bfloat16)
    grad_output = contract_rows(attended, branch_low)
    grad_attended = contract_cols(branch_low, full_output).astype(jnp.bfloat16)
    grad_queries, grad_keys, grad_values, grad_table_all = attention_backward(
        queries,
        keys_all,
        values_all,
        log_totals,
        grad_attended,
        table_pair(full_rel, full_lay),
        onehot,
        valid,
    )
    grad_rel = grad_table_all[:NB].reshape(NB * H)
    grad_lay = grad_table_all[NB:].reshape(NB * H)
    grad_query = contract_rows(normed_attn, grad_queries)
    grad_key = contract_rows(normed_attn, grad_keys)
    grad_value = contract_rows(normed_attn, grad_values)
    grad_normed_attn = (
        contract_cols(grad_queries, full_query)
        + contract_cols(grad_keys, full_key)
        + contract_cols(grad_values, full_value)
    )
    input_value, input_pull = jax.vjp(rms_scale, tokens_f, full_gain_attn.astype(jnp.float32))
    grad_input_part, grad_gain_attn = input_pull(grad_normed_attn)
    grad_tokens = grad_hidden + grad_input_part
    owned = (
        lax.psum_scatter(grad_query, ("wide", "narrow"), scatter_dimension=0, tiled=True),
        lax.psum_scatter(grad_key, ("wide", "narrow"), scatter_dimension=0, tiled=True),
        lax.psum_scatter(grad_value, ("wide", "narrow"), scatter_dimension=0, tiled=True),
        lax.psum_scatter(grad_output, ("wide", "narrow"), scatter_dimension=0, tiled=True),
        lax.psum_scatter(grad_gate, ("wide", "narrow"), scatter_dimension=0, tiled=True),
        lax.psum_scatter(grad_up, ("wide", "narrow"), scatter_dimension=0, tiled=True),
        lax.psum_scatter(grad_down, ("wide", "narrow"), scatter_dimension=0, tiled=True),
        lax.psum_scatter(grad_gain_attn, ("wide", "narrow"), scatter_dimension=0, tiled=True),
        lax.psum_scatter(grad_gain_ffn, ("wide", "narrow"), scatter_dimension=0, tiled=True),
        lax.psum_scatter(grad_rel, ("wide", "narrow"), scatter_dimension=0, tiled=True),
        lax.psum_scatter(grad_lay, ("wide", "narrow"), scatter_dimension=0, tiled=True),
    )
    return (
        output,
        grad_tokens,
        owned[0],
        owned[1],
        owned[2],
        owned[3],
        owned[4],
        owned[5],
        owned[6],
        owned[7],
        owned[8],
        owned[9],
        owned[10],
    )


def solution(mesh):
    nw, nn = mesh.shape["wide"], mesh.shape["narrow"]

    def body(*args):
        if nw == 8 and nw * nn == NB and args[1].shape[0] % 16 == 0:
            return local_fast(nw, nn, *args)
        return local(*args)

    placed = (
        P(("wide", "narrow"), None),
        P(("wide", "narrow"), None),
        P(("wide", "narrow"), None),
        P(("wide", "narrow"), None),
        P(("wide", "narrow"), None),
        P(("wide", "narrow"), None),
        P(("wide", "narrow"), None),
        P(("wide", "narrow"), None),
        P(("wide", "narrow")),
        P(("wide", "narrow")),
        P(("wide", "narrow")),
        P(("wide", "narrow")),
        P(("wide", "narrow")),
        P(("wide", "narrow"), None),
        P(("wide", "narrow"), None),
        P(("wide", "narrow"), None),
    )
    return jax.shard_map(
        body,
        mesh=mesh,
        in_specs=placed,
        out_specs=(
            P(("wide", "narrow"), None),
            P(("wide", "narrow"), None),
            P(("wide", "narrow"), None),
            P(("wide", "narrow"), None),
            P(("wide", "narrow"), None),
            P(("wide", "narrow"), None),
            P(("wide", "narrow"), None),
            P(("wide", "narrow"), None),
            P(("wide", "narrow"), None),
            P(("wide", "narrow")),
            P(("wide", "narrow")),
            P(("wide", "narrow")),
            P(("wide", "narrow")),
        ),
        check_vma=False,
    )
```

profile of v0, /device:TPU:0, one launch (start us, length us, event | category | flops | bytes accessed | tf_op | source)
XLA Modules:
  0.0 259.3 jit_solution(18416929188391350344)
XLA Ops:
  1.3 1.4 fusion.9.refs_5_
  2.7 1.6 pad.12.refs_12_
  4.3 122.2 %shard_map.255 = (f32[256,128]{1,0:T(8,128)}, bf16[1024,1024]{1,0:T(8,128)(2,1)}, bf16[1024,1024]{1,0:T(8,128)(2,1)}, bf16[1024,1024]{1,0:T(8,128)(2,1)}, bf16[1...) custom-call(s32[1]{0:T(128)S(6)} %copy.29.refs_0_, ...), custom_call_target="tpu_custom_call" | custom-call | tf_op jit(solution)/shard_map/pallas_call | solution.py:964
  126.5 127.3 %shard_map.256 = (bf16[512,1024]{1,0:T(8,128)(2,1)}, f32[512,1024]{1,0:T(8,128)}, f32[4,88,256]{2,1,0:T(8,128)}, f32[19,32,512]{2,1,0:T(8,128)}, f32[8,128]{1,0:...) custom-call(s32[1]{0:T(128)S(6)} %copy.29.refs_0_, bf16[512,1024]{1,0:T(8,128)(2,1)} %refs_1_.3, ...), custom_call_target="tpu_custom_call" | custom-call | tf_op jit(solution)/shard_map/pallas_call | solution.py:1902
  253.8 5.4 %shard_map.257 = (bf16[512,1024]{1,0:T(8,128)(2,1)}, f32[512,1024]{1,0:T(8,128)}, f32[32,1024]{1,0:T(8,128)}, f32[32,1024]{1,0:T(8,128)}, f32[32,1024]{1,0:T(8,1...) custom-call(f32[4,88,256]{2,1,0:T(8,128)} %get-tuple-element.62.few_, ...), custom_call_target="tpu_custom_call" | custom-call | tf_op jit(solution)/shard_map/pallas_call | solution.py:2021
where the time goes:
time: 260 us; the launch traced here: 259 us
  Pallas kernels  255 us (98%)
    pallas_call x1, Pallas kernels, backward_all(): pl.pallas_call(functools.partial(backward_kernel, nn, few, many), out_sha...  127 us
    pallas_call x1, Pallas kernels, forward_all(): pl.pallas_call(functools.partial(forward_kernel, nn, shapes), out_shape=o...  122 us
    pallas_call x1, Pallas kernels, place_all(): pl.pallas_call(place_kernel, out_shape=outs, in_specs=[hbm] * 4 + [vmem],...  5.37 us

commit v1 on v0

--- a/solution.py
+++ b/solution.py
@@ -23,6 +23,7 @@
 WIDE = 512
 DOWN_PIECE = 256
 REST = 512
+FIRST = 512
 UP_TILES = 6
 TILE = 256
 QB = 8
@@ -495,21 +496,26 @@
     return jnp.where(mask, 1.0, 0.0).astype(BF)
 
 
-def unpack_row(rows, first, each, total):
+def small_rows(small, index):
+    return small.reshape(small.shape[0] // 8, 8, 128)[:, index, :]
+
+
+def unpack_row(small, index, total):
+    rows = small_rows(small, index)
     devices = rows.shape[0]
-    pick = ones_where(iota((128, total), 0) == first + lax.rem(iota((128, total), 1), each))
+    each = total // devices
+    pick = ones_where(iota((128, total), 0) == lax.rem(iota((128, total), 1), each))
     spread = dot(rows.astype(BF), pick)
     mine = iota((devices, total), 1) // each == iota((devices, total), 0)
     return jnp.sum(jnp.where(mine, spread, 0.0), axis=0, keepdims=True)
 
 
-def table_block(rows, first):
+def table_block(small):
     pick_shape = (H * QB, 128)
     total = None
+    pick = ones_where(iota(pick_shape, 1) == iota(pick_shape, 0) // QB)
     for index in range(2):
-        lane = first + H * index + iota(pick_shape, 0) // QB
-        pick = ones_where(iota(pick_shape, 1) == lane)
-        table = dot_nt(pick, rows.astype(BF)).astype(BF)
+        table = dot_nt(pick, small_rows(small, 2 + index).astype(BF)).astype(BF)
         wide = (NB, QB * 2 * NB)
         spread = dot(table, ones_where(lax.rem(iota(wide, 1), 2 * NB) == iota(wide, 0) + NB * index))
         total = spread if total is None else total + spread
@@ -531,8 +537,9 @@
 def forward_kernel(nn, shapes, *refs):
     count = len(shapes)
     occupied, tokens, rel_hbm, lay_hbm, cotangent = refs[:5]
-    shards = refs[5 : 5 + count]
-    refs = refs[5 + count :]
+    parameters, down_shard = refs[5:9], refs[9]
+    shards = refs[10 : 8 + count]
+    refs = refs[8 + count :]
     fulls, refs = refs[:count], refs[count:]
     (grad_h, na_t, q_t, k_h, v_h, att_t, hid_h, nf_t, mix_h, probs_h, slope_h, act_h) = refs[:12]
     down_grads, down_came, refs = refs[12], refs[13], refs[14:]
@@ -573,7 +580,10 @@
         rest_lines,
         rest_merged,
         rest_sem,
+        small_shard,
+        down_padded,
     ) = refs
+    shards = (small_shard,) + tuple(shards) + (down_padded,)
     slots, width = x.shape
     links = Links(nn, send_sem, recv_sem)
     numbers = iter(range(64))
@@ -583,23 +593,27 @@
         copy.start()
         return copy
 
-    arriving = [move(tokens, x), move(rel_hbm, rel), move(lay_hbm, lay)]
-    grad_in = move(cotangent, grad)
+    small_shard[...] = jnp.zeros_like(small_shard)
+    for index, part in enumerate(parameters):
+        small_shard[index : index + 1, : part.shape[0]] = part[...].astype(F32).reshape(1, part.shape[0])
+    down_padded[...] = jnp.zeros_like(down_padded)
+    down_padded[: down_shard.shape[0], :] = down_shard[...]
     links.greet()
     g = []
-    first_up = UP_TILES * TILE
-    cuts = [(0, columns) for rows, columns in shapes]
-    cuts[6:] = [(0, first_up), (first_up, shapes[6][1] - first_up), (0, width - REST)]
-    for number, (low, columns) in enumerate(cuts):
-        index = min(number, 6) if number < 8 else 7
-        rows = shapes[index][0]
+    first, wide = UP_TILES * TILE, shapes[5][1]
+    cuts = [(0, 0, shapes[0][1]), (1, 0, FIRST), (1, FIRST, width - FIRST)]
+    cuts += [(index, 0, width) for index in (2, 3, 4)]
+    for index in (5, 6):
+        cuts += [(index, 0, first), (index, first, wide - first)]
+    cuts.append((7, 0, width - REST))
+    for number, (index, low, columns) in enumerate(cuts):
         odd = index == 7
         g.append(
             Gather(
                 links,
                 shards[index].at[:, pl.ds(low, columns)],
                 w_wide.at[index - 5] if index in (5, 6) else fulls[index],
-                rows,
+                shapes[index][0],
                 (low, columns),
                 halves(columns, low) if columns > 128 else ((0, columns, PARTS[0]),),
                 gather_sem.at[number],
@@ -620,7 +634,7 @@
         rest_merged,
     )
     down_id = links.used
-    small_g, q_g, k_g, v_g, o_g, gate_g, up_g, up_two_g, down_g = g
+    small_g, q_g, q_two_g, k_g, v_g, o_g, gate_g, gate_two_g, up_g, up_two_g, down_g = g
     leaving = []
     turning = {}
     ffn = mixed_t.shape[0]
@@ -646,11 +660,9 @@
         turning[slot] = move(turned.at[slot], target)
 
     def unpack():
-        rows = small.reshape(small.shape[0] // 8, 8, 128)[:, 0, :]
-        each = width // rows.shape[0]
-        gains[0:1, :] = unpack_row(rows, 0, each, width)
-        gains[1:2, :] = unpack_row(rows, each, each, width)
-        lhs[...] = table_block(rows, 2 * each)
+        gains[0:1, :] = unpack_row(small, 0, width)
+        gains[1:2, :] = unpack_row(small, 1, width)
+        lhs[...] = table_block(small)
 
     def normalise(source, row, target):
         def one(index, carry):
@@ -814,80 +826,96 @@
 
     small_g.start()
     q_g.start()
+    q_two_g.start()
     rest.start()
+    arriving = [move(tokens, x), move(rel_hbm, rel), move(lay_hbm, lay)]
+    grad_in = move(cotangent, grad)
+    q_g.ready()
+    q_g.spread()
+    k_g.start()
     small_g.ready()
     small_g.spread()
-    k_g.start()
-    q_g.ready()
-    q_g.spread()
+    q_two_g.ready()
+    q_two_g.spread()
     v_g.start()
     small_g.forward()
+    q_g.forward()
     small_g.settle()
     small_g.last()
     small_g.done()
     small_in = move(fulls[0], small)
     rest.forward()
-    for copy in arriving:
-        copy.wait()
     k_g.ready()
     k_g.spread()
     o_g.start()
     gate_g.start()
-    q_g.forward()
+    q_two_g.forward()
+    for copy in arriving:
+        copy.wait()
     small_in.wait()
     unpack()
     normalise(x, 0, na)
     turn_out(0, na, na_t)
     q_g.settle()
+    q_two_g.settle()
     add_bias(0, 4)
     v_g.ready()
     v_g.spread()
     k_g.forward()
     q_g.last()
+    q_two_g.last()
     add_bias(1, 4)
     k_g.settle()
     o_g.ready()
     o_g.spread()
-    up_g.start()
+    gate_two_g.start()
     v_g.forward()
     add_bias(2, 4)
     k_g.last()
     v_g.settle()
     q_g.done()
+    q_two_g.done()
     fetch_q = move(fulls[1], w_one.at[0])
-    add_bias(3, 4)
     gate_g.ready()
     gate_g.spread()
-    up_two_g.start()
+    up_g.start()
     o_g.forward()
+    add_bias(3, 4)
     fetch_q.wait()
     project(0, q)
     turn_out(1, q, q_t)
     k_g.done()
     fetch_k = move(fulls[2], w_one.at[1])
     v_g.last()
+    gate_two_g.ready()
+    gate_two_g.spread()
+    up_two_g.start()
     fetch_k.wait()
     project(1, k)
     leaving.append(move(k, k_h))
     v_g.done()
     fetch_v = move(fulls[3], w_one.at[0])
+    gate_g.forward()
     o_g.settle()
+    o_g.last()
     fetch_v.wait()
     project(0, v)
     leaving.append(move(v, v_h))
+    o_g.done()
+    fetch_o = move(fulls[4], w_one.at[1])
     attend(0, 3)
+    gate_two_g.forward()
     up_g.ready()
     up_g.spread()
     down_g.start()
-    o_g.last()
-    gate_g.forward()
-    o_g.done()
-    fetch_o = move(fulls[4], w_one.at[1])
+    gate_g.settle()
     attend(3, 6)
-    gate_g.settle()
-    rest.line()
+    gate_g.last()
+    gate_two_g.settle()
     attend(6, pairs)
     turn_out(0, att, att_t)
+    down_g.ready()
+    rest.line()
     fetch_o.wait()
     output()
     normalise(hid, 1, nf)
@@ -895,14 +923,15 @@
     up_g.forward()
     up_two_g.ready()
     up_two_g.spread()
+    gate_two_g.last()
+    gate_g.done()
     grad_in.wait()
     keep_valid()
-    down_g.ready()
+    lax.fori_loop(0, UP_TILES, gate_tile, 0)
     up_g.settle()
-    gate_g.last()
-    gate_g.done()
+    gate_two_g.done()
     leaving.append(move(w_wide.at[0], fulls[5]))
-    lax.fori_loop(0, tiles, gate_tile, 0)
+    lax.fori_loop(UP_TILES, tiles, gate_tile, 0)
     up_g.last()
     up_two_g.forward()
     down_g.spread()
@@ -911,14 +940,14 @@
     up_two_g.settle()
     down_units(0, chunks)
     up_two_g.last()
-    down_g.forward()
-    down_g.settle()
     up_two_g.done()
     leaving.append(move(w_wide.at[1], fulls[6]))
     lax.fori_loop(UP_TILES, tiles, ffn_tile, 0)
+    down_g.forward()
+    down_units(chunks, 2 * chunks)
+    down_g.settle()
+    rest.join()
     down_g.last()
-    rest.join()
-    down_units(chunks, 2 * chunks)
     down_copy(jnp.int32(2 * chunks - 1)).wait()
     down_trade(jnp.int32(2 * chunks - 1)).start()
     down_g.done()
@@ -935,21 +964,20 @@
     links.finish()
 
 
-def forward_all(nw, nn, counts, tokens, rel, lay, cotangent, shards, odd_rows):
+def forward_all(nw, nn, counts, tokens, rel, lay, cotangent, parameters, shards):
     devices = nw * nn
-    shapes = []
-    for index, shard in enumerate(shards):
-        rows = odd_rows if index == len(shards) - 1 else shard.shape[0]
-        shapes.append((rows, shard.shape[1]))
+    shapes = [(8, 128)] + [shard.shape for shard in shards]
+    odd_rows = shards[-1].shape[0]
+    tile_rows = padded(odd_rows)
     slots, width = tokens.shape
-    copies = (len(shards) + 2) * (nn - 1 + 6 + nw // 2) + 2 * (width // DOWN_PIECE)
+    copies = (len(shapes) + 4) * (nn - 1 + 6 + nw // 2) + 2 * (width // DOWN_PIECE)
     ffn = shapes[5][1]
     low = jax.ShapeDtypeStruct((slots, width), BF)
     wide = jax.ShapeDtypeStruct((slots, ffn), BF)
     full = jax.ShapeDtypeStruct((slots, width), F32)
     out_shape = [
-        jax.ShapeDtypeStruct((rows * devices, columns), shard.dtype)
-        for (rows, columns), shard in zip(shapes, shards)
+        jax.ShapeDtypeStruct((rows * devices, columns), BF if index else F32)
+        for index, (rows, columns) in enumerate(shapes)
     ]
     low_t = jax.ShapeDtypeStruct((width, slots), BF)
     out_shape += [low, low_t, low_t, low, low, low_t, full, low_t, wide]
@@ -957,14 +985,16 @@
     down = (nw // 2, 2, nn * odd_rows, DOWN_PIECE)
     out_shape += [jax.ShapeDtypeStruct((width // DOWN_PIECE,) + down, BF)]
     out_shape += [jax.ShapeDtypeStruct((width // DOWN_PIECE, nw // 2, nn * odd_rows, DOWN_PIECE), BF)]
-    tile_rows = shards[-1].shape[0]
     half = (tile_rows, REST)
     hbm = pl.BlockSpec(memory_space=pl.ANY)
     page = pltpu.VMEM((slots, width), BF)
     return pl.pallas_call(
         functools.partial(forward_kernel, nn, shapes),
         out_shape=out_shape,
-        in_specs=[pl.BlockSpec(memory_space=pltpu.SMEM)] + [hbm] * (4 + len(shards)),
+        in_specs=[pl.BlockSpec(memory_space=pltpu.SMEM)]
+        + [hbm] * 4
+        + [pl.BlockSpec(memory_space=pltpu.VMEM)] * 5
+        + [hbm] * (len(shards) - 1),
         out_specs=[hbm] * len(out_shape),
         scratch_shapes=[
             pltpu.VMEM((nn, tile_rows, width - REST), BF),
@@ -996,18 +1026,20 @@
             pltpu.VMEM((ffn, slots), BF),
             pltpu.SemaphoreType.DMA((copies,)),
             pltpu.SemaphoreType.DMA((copies,)),
-            pltpu.SemaphoreType.DMA((len(shards) + 1,)),
+            pltpu.SemaphoreType.DMA((len(shapes) + 3,)),
             pltpu.SemaphoreType.DMA((64,)),
             pltpu.SemaphoreType.DMA((10,)),
             pltpu.VMEM((nw // 2,) + half, BF),
             pltpu.VMEM((nn, nw // 2) + half, BF),
             pltpu.VMEM((nw // 2, nn * odd_rows, half[1]), BF),
             pltpu.SemaphoreType.DMA((1 + nw // 2,)),
+            pltpu.VMEM((8, 128), F32),
+            pltpu.VMEM((tile_rows, width), BF),
         ],
         compiler_params=pltpu.CompilerParams(
             collective_id=0, has_side_effects=True, vmem_limit_bytes=63 * 2**20
         ),
-    )(counts, tokens, rel, lay, cotangent, *shards)
+    )(counts, tokens, rel, lay, cotangent, *parameters, shards[-1], *shards[:-1])
 
 
 class Scatter:
@@ -1465,7 +1497,6 @@
     tiles = ffn // TILE
     pairs = H // 2
     wide = many.columns
-    squares = many_stage.shape[1]
     devices = small.shape[0] // 8
     each = width // devices
     zero = jnp.zeros((8, width), F32)
@@ -1488,7 +1519,8 @@
 
     def many_copy(chunk):
         turn = lax.rem(chunk, 2)
-        return pltpu.make_async_copy(many_stage.at[turn], many.grads.at[chunk], stage_sem.at[turn])
+        place = many.grads.at[chunk]
+        return pltpu.make_async_copy(many_stage.at[turn].reshape(place.shape), place, stage_sem.at[turn])
 
     def flush(chunk):
         many_copy(chunk).wait()
@@ -1496,7 +1528,7 @@
 
     def make(chunk, left_rows, right, dot_one):
         found = dot_one(left_rows[...], right())
-        many_stage[lax.rem(chunk, 2)] = found.astype(BF).reshape(many_stage.shape[1:])
+        many_stage[lax.rem(chunk, 2)] = found.astype(BF)
         many_copy(chunk).start()
 
     def few_pump(index):
@@ -1513,10 +1545,8 @@
             for copy in tile_copies(tile + 1):
                 copy.start()
 
-        @pl.when(tile == 3)
-        def _():
-            start(*later)
-            start(*last)
+        for number, copy in enumerate(later + last):
+            pl.when(tile == 3 + number // 2)(copy.start)
 
         for copy in tile_copies(tile):
             copy.wait()
@@ -1544,9 +1574,8 @@
         return carry
 
     def unpack():
-        rows = small.reshape(devices, 8, 128)[:, 0, :]
-        gains[0:1, :] = unpack_row(rows, 0, each, width)
-        gains[1:2, :] = unpack_row(rows, each, each, width)
+        gains[0:1, :] = unpack_row(small, 0, width)
+        gains[1:2, :] = unpack_row(small, 1, width)
 
     def norm_two():
         def one(index, total):
@@ -1929,7 +1958,7 @@
             pltpu.VMEM((slots, 2 * TILE), BF),
             pltpu.VMEM((2, slots, TILE), BF),
             pltpu.VMEM((2, slots, TILE), BF),
-            pltpu.VMEM((2, squares, 2, nn * many[1], many[2]), BF),
+            pltpu.VMEM((2, width, many[2]), BF),
             low,
             pltpu.VMEM((2, width, width), BF),
             low,
@@ -2055,13 +2084,12 @@
     lay_bucket,
     cotangent,
 ):
-    small = jnp.concatenate([gain_attn, gain_ffn, rel_table, lay_table]).astype(F32)
-    small = jnp.pad(small[None], ((0, 7), (0, 128 - small.shape[0])))
-    down = jnp.pad(w_down, ((0, padded(w_down.shape[0]) - w_down.shape[0]), (0, 0)))
     page = (tokens, rel_bucket, lay_bucket)
-    shards = [small, w_query, w_key, w_value, w_output, w_gate, w_up, down]
-    found = forward_all(nw, nn, ocr_counts, *page, cotangent, shards, w_down.shape[0])
-    weights, grad, saved = found[: len(shards)], found[len(shards)], found[len(shards) + 1 :]
+    parameters = (gain_attn, gain_ffn, rel_table, lay_table)
+    shards = (w_query, w_key, w_value, w_output, w_gate, w_up, w_down)
+    found = forward_all(nw, nn, ocr_counts, *page, cotangent, parameters, shards)
+    count = 1 + len(shards)
+    weights, grad, saved = found[:count], found[count], found[count + 1 :]
     output, grad_tokens, few, many, small = backward_all(
         nw, nn, ocr_counts, page + (grad,), weights, saved
     )

time: 260 us -> 248 us (0.954)
  Pallas kernels: 255 us -> 246 us
    pallas_call x1, Pallas kernels: 127 us -> 121 us  [backward_all(): pl.pallas_call(functools.partial(backward_kernel, nn, few, many), out_sha...]
    pallas_call x1, Pallas kernels: 122 us -> 119 us  [forward_all(): pl.pallas_call(functools.partial(forward_kernel, nn, shapes), out_shape=o...]
where the time goes in v1:
time: 248 us; the launch traced here: 247 us
  Pallas kernels  246 us (99%)
    pallas_call x1, Pallas kernels, backward_all(): pl.pallas_call(functools.partial(backward_kernel, nn, few, many), out_sha...  121 us
    pallas_call x1, Pallas kernels, forward_all(): pl.pallas_call(functools.partial(forward_kernel, nn, shapes), out_shape=o...  119 us
    pallas_call x1, Pallas kernels, place_all(): pl.pallas_call(place_kernel, out_shape=outs, in_specs=[hbm] * 4 + [vmem],...  5.37 us

profile of v1, /device:TPU:0, one launch (start us, length us, event | category | flops | bytes accessed | tf_op | source)
XLA Modules:
  0.0 247.5 jit_solution(13656404624359628105)
XLA Ops:
  1.3 119.4 %shard_map.255 = (f32[256,128]{1,0:T(8,128)}, bf16[1024,1024]{1,0:T(8,128)(2,1)}, bf16[1024,1024]{1,0:T(8,128)(2,1)}, bf16[1024,1024]{1,0:T(8,128)(2,1)}, bf16[1...) custom-call(s32[1]{0:T(128)S(6)} %copy.29.refs_0_, ...), custom_call_target="tpu_custom_call" | custom-call | tf_op jit(solution)/shard_map/pallas_call | solution.py:991
  120.7 121.3 %shard_map.256 = (bf16[512,1024]{1,0:T(8,128)(2,1)}, f32[512,1024]{1,0:T(8,128)}, f32[4,88,256]{2,1,0:T(8,128)}, f32[19,32,512]{2,1,0:T(8,128)}, f32[8,128]{1,0:...) custom-call(s32[1]{0:T(128)S(6)} %copy.29.refs_0_, bf16[512,1024]{1,0:T(8,128)(2,1)} %refs_1_.3, ...), custom_call_target="tpu_custom_call" | custom-call | tf_op jit(solution)/shard_map/pallas_call | solution.py:1931
  241.9 5.4 %shard_map.257 = (bf16[512,1024]{1,0:T(8,128)(2,1)}, f32[512,1024]{1,0:T(8,128)}, f32[32,1024]{1,0:T(8,128)}, f32[32,1024]{1,0:T(8,128)}, f32[32,1024]{1,0:T(8,1...) custom-call(f32[4,88,256]{2,1,0:T(8,128)} %get-tuple-element.62.few_, ...), custom_call_target="tpu_custom_call" | custom-call | tf_op jit(solution)/shard_map/pallas_call | solution.py:2050

commit v2 on v1

--- a/solution.py
+++ b/solution.py
@@ -234,6 +234,8 @@
 X_BIT = 2
 Y_BIT = 4
 PARTS = ((X_BIT, Y_BIT), (Y_BIT, X_BIT))
+NEAR = 1
+FAR = 2
 
 
 class Links:
@@ -255,6 +257,9 @@
 
     def along(self, step):
         return (self.w, lax.rem(self.z + step, self.nn))
+
+    def line(self, bit):
+        return (self.w, jnp.bitwise_xor(self.z, bit))
 
     def copy(self, src, dst, number, device):
         return pltpu.make_async_remote_copy(
@@ -317,17 +322,24 @@
     def start(self):
         k = self.links
         self.own().start()
-        for step in range(1, k.nn):
-            k.send(self.shard, self.place(k.w, k.z), self.line_ids[step - 1], k.along(step))
+        for bit in (FAR, NEAR):
+            k.send(self.shard, self.place(k.w, k.z), self.line_ids[bit - 1], k.line(bit))
+
+    def landed(self, bit):
+        k = self.links
+        place = self.place(k.w, jnp.bitwise_xor(k.z, bit))
+        k.copy(place, place, self.line_ids[bit - 1], k.line(NEAR)).wait_recv()
+        return place
+
+    def middle(self):
+        place = self.landed(FAR)
+        self.links.send(place, place, self.line_ids[2], self.links.line(NEAR))
 
     def ready(self):
+        self.own().wait()
+        self.landed(NEAR)
+        self.landed(NEAR | FAR)
         k = self.links
-        self.own().wait()
-        for step in range(1, k.nn):
-            came = lax.rem(k.z - step + k.nn, k.nn)
-            k.copy(
-                self.shard, self.place(k.w, came), self.line_ids[step - 1], k.along(step)
-            ).wait_recv()
         if self.line is not None:
             whole = jnp.concatenate(
                 [self.line[z, : self.rows].astype(F32) for z in range(k.nn)], axis=0
@@ -435,8 +447,18 @@
         for p in range(len(self.parts)):
             self.arrive(p, X_BIT | Y_BIT)
         self.keep().start()
-        for step in range(1, k.nn):
-            k.send(self.square, self.lines.at[k.z], self.line_ids[step - 1], k.along(step))
+        for bit in (FAR, NEAR):
+            k.send(self.square, self.lines.at[k.z], self.line_ids[bit - 1], k.line(bit))
+
+    def landed(self, bit):
+        k = self.links
+        place = self.lines.at[jnp.bitwise_xor(k.z, bit)]
+        k.copy(place, place, self.line_ids[bit - 1], k.line(NEAR)).wait_recv()
+        return place
+
+    def middle(self):
+        place = self.landed(FAR)
+        self.links.send(place, place, self.line_ids[2], self.links.line(NEAR))
 
     def rows_of(self, square, core):
         rows = pl.ds((square * 2 + core) * self.block, self.block)
@@ -451,9 +473,8 @@
     def join(self):
         k = self.links
         self.keep().wait()
-        for step in range(1, k.nn):
-            came = lax.rem(k.z - step + k.nn, k.nn)
-            k.copy(self.square, self.lines.at[came], self.line_ids[step - 1], k.along(step)).wait_recv()
+        self.landed(NEAR)
+        self.landed(NEAR | FAR)
 
         def one(square, carry):
             whole = jnp.concatenate(
@@ -582,6 +603,10 @@
         rest_sem,
         small_shard,
         down_padded,
+        o_square,
+        o_lines,
+        o_merged,
+        o_sem,
     ) = refs
     shards = (small_shard,) + tuple(shards) + (down_padded,)
     slots, width = x.shape
@@ -602,7 +627,7 @@
     g = []
     first, wide = UP_TILES * TILE, shapes[5][1]
     cuts = [(0, 0, shapes[0][1]), (1, 0, FIRST), (1, FIRST, width - FIRST)]
-    cuts += [(index, 0, width) for index in (2, 3, 4)]
+    cuts += [(index, 0, width) for index in (2, 3)]
     for index in (5, 6):
         cuts += [(index, 0, first), (index, first, wide - first)]
     cuts.append((7, 0, width - REST))
@@ -633,8 +658,11 @@
         rest_lines,
         rest_merged,
     )
+    o_g = GatherSquare(
+        links, shards[4], fulls[4], shapes[4][0], (0, width), o_sem, o_square, o_lines, o_merged
+    )
     down_id = links.used
-    small_g, q_g, q_two_g, k_g, v_g, o_g, gate_g, gate_two_g, up_g, up_two_g, down_g = g
+    small_g, q_g, q_two_g, k_g, v_g, gate_g, gate_two_g, up_g, up_two_g, down_g = g
     leaving = []
     turning = {}
     ffn = mixed_t.shape[0]
@@ -827,16 +855,21 @@
     small_g.start()
     q_g.start()
     q_two_g.start()
+    o_g.start()
     rest.start()
     arriving = [move(tokens, x), move(rel_hbm, rel), move(lay_hbm, lay)]
     grad_in = move(cotangent, grad)
+    small_g.middle()
+    q_g.middle()
+    q_two_g.middle()
+    k_g.start()
     q_g.ready()
     q_g.spread()
-    k_g.start()
     small_g.ready()
     small_g.spread()
     q_two_g.ready()
     q_two_g.spread()
+    k_g.middle()
     v_g.start()
     small_g.forward()
     q_g.forward()
@@ -844,10 +877,11 @@
     small_g.last()
     small_g.done()
     small_in = move(fulls[0], small)
+    o_g.forward()
     rest.forward()
     k_g.ready()
     k_g.spread()
-    o_g.start()
+    v_g.middle()
     gate_g.start()
     q_two_g.forward()
     for copy in arriving:
@@ -858,71 +892,74 @@
     turn_out(0, na, na_t)
     q_g.settle()
     q_two_g.settle()
-    add_bias(0, 4)
     v_g.ready()
     v_g.spread()
     k_g.forward()
+    gate_g.middle()
+    gate_two_g.start()
     q_g.last()
     q_two_g.last()
+    add_bias(0, 4)
+    k_g.settle()
+    gate_g.ready()
+    gate_g.spread()
+    gate_two_g.middle()
+    up_g.start()
+    v_g.forward()
     add_bias(1, 4)
-    k_g.settle()
-    o_g.ready()
-    o_g.spread()
-    gate_two_g.start()
-    v_g.forward()
-    add_bias(2, 4)
     k_g.last()
-    v_g.settle()
     q_g.done()
     q_two_g.done()
     fetch_q = move(fulls[1], w_one.at[0])
-    gate_g.ready()
-    gate_g.spread()
-    up_g.start()
-    o_g.forward()
+    v_g.settle()
+    up_g.middle()
+    up_two_g.start()
+    add_bias(2, 4)
+    k_g.done()
+    fetch_k = move(fulls[2], w_one.at[1])
+    gate_two_g.ready()
+    gate_two_g.spread()
+    gate_g.forward()
+    up_two_g.middle()
+    o_g.line()
     add_bias(3, 4)
+    v_g.last()
     fetch_q.wait()
     project(0, q)
     turn_out(1, q, q_t)
-    k_g.done()
-    fetch_k = move(fulls[2], w_one.at[1])
-    v_g.last()
-    gate_two_g.ready()
-    gate_two_g.spread()
-    up_two_g.start()
+    v_g.done()
+    fetch_v = move(fulls[3], w_one.at[0])
     fetch_k.wait()
     project(1, k)
     leaving.append(move(k, k_h))
-    v_g.done()
-    fetch_v = move(fulls[3], w_one.at[0])
-    gate_g.forward()
-    o_g.settle()
-    o_g.last()
     fetch_v.wait()
     project(0, v)
     leaving.append(move(v, v_h))
-    o_g.done()
-    fetch_o = move(fulls[4], w_one.at[1])
+    up_g.ready()
+    up_g.spread()
+    gate_g.settle()
     attend(0, 3)
     gate_two_g.forward()
-    up_g.ready()
-    up_g.spread()
+    o_g.middle()
     down_g.start()
-    gate_g.settle()
     attend(3, 6)
     gate_g.last()
     gate_two_g.settle()
     attend(6, pairs)
     turn_out(0, att, att_t)
+    o_g.join()
+    down_g.middle()
+    up_g.forward()
+    up_two_g.ready()
+    up_two_g.spread()
+    o_g.done()
+    fetch_o = move(fulls[4], w_one.at[1])
     down_g.ready()
     rest.line()
     fetch_o.wait()
     output()
     normalise(hid, 1, nf)
     turn_out(1, nf, nf_t)
-    up_g.forward()
-    up_two_g.ready()
-    up_two_g.spread()
     gate_two_g.last()
     gate_g.done()
     grad_in.wait()
@@ -939,6 +976,7 @@
     lax.fori_loop(0, UP_TILES, ffn_tile, 0)
     up_two_g.settle()
     down_units(0, chunks)
+    rest.middle()
     up_two_g.last()
     up_two_g.done()
     leaving.append(move(w_wide.at[1], fulls[6]))
@@ -1035,6 +1073,10 @@
             pltpu.SemaphoreType.DMA((1 + nw // 2,)),
             pltpu.VMEM((8, 128), F32),
             pltpu.VMEM((tile_rows, width), BF),
+            pltpu.VMEM((nw // 2,) + shards[3].shape, BF),
+            pltpu.VMEM((nn, nw // 2) + shards[3].shape, BF),
+            pltpu.VMEM((nw // 2, nn * shards[3].shape[0], width), BF),
+            pltpu.SemaphoreType.DMA((1 + nw // 2,)),
         ],
         compiler_params=pltpu.CompilerParams(
             collective_id=0, has_side_effects=True, vmem_limit_bytes=63 * 2**20

time: 248 us -> 243 us (0.980)
  Pallas kernels: 246 us -> 241 us
    pallas_call x1, Pallas kernels: 121 us -> 118 us  [backward_all(): pl.pallas_call(functools.partial(backward_kernel, nn, few, many), out_sha...]
where the time goes in v2:
time: 243 us
  Pallas kernels  241 us (99%)
    pallas_call x1, Pallas kernels, backward_all(): pl.pallas_call(functools.partial(backward_kernel, nn, few, many), out_sha...  118 us
    pallas_call x1, Pallas kernels, forward_all(): pl.pallas_call(functools.partial(forward_kernel, nn, shapes), out_shape=o...  118 us
    pallas_call x1, Pallas kernels, place_all(): pl.pallas_call(place_kernel, out_shape=outs, in_specs=[hbm] * 4 + [vmem],...  5.37 us

profile of v2, /device:TPU:0, one launch (start us, length us, event | category | flops | bytes accessed | tf_op | source)
XLA Modules:
  0.0 242.8 jit_solution(2760450106347376641)
XLA Ops:
  1.3 117.7 %shard_map.255 = (f32[256,128]{1,0:T(8,128)}, bf16[1024,1024]{1,0:T(8,128)(2,1)}, bf16[1024,1024]{1,0:T(8,128)(2,1)}, bf16[1024,1024]{1,0:T(8,128)(2,1)}, bf16[1...) custom-call(s32[1]{0:T(128)S(6)} %copy.29.refs_0_, ...), custom_call_target="tpu_custom_call" | custom-call | tf_op jit(solution)/shard_map/pallas_call | solution.py:1029
  119.0 118.3 %shard_map.256 = (bf16[512,1024]{1,0:T(8,128)(2,1)}, f32[512,1024]{1,0:T(8,128)}, f32[4,88,256]{2,1,0:T(8,128)}, f32[19,32,512]{2,1,0:T(8,128)}, f32[8,128]{1,0:...) custom-call(s32[1]{0:T(128)S(6)} %copy.29.refs_0_, bf16[512,1024]{1,0:T(8,128)(2,1)} %refs_1_.3, ...), custom_call_target="tpu_custom_call" | custom-call | tf_op jit(solution)/shard_map/pallas_call | solution.py:1973
  237.3 5.4 %shard_map.257 = (bf16[512,1024]{1,0:T(8,128)(2,1)}, f32[512,1024]{1,0:T(8,128)}, f32[32,1024]{1,0:T(8,128)}, f32[32,1024]{1,0:T(8,128)}, f32[32,1024]{1,0:T(8,1...) custom-call(f32[4,88,256]{2,1,0:T(8,128)} %get-tuple-element.62.few_, ...), custom_call_target="tpu_custom_call" | custom-call | tf_op jit(solution)/shard_map/pallas_call | solution.py:2092
